TPU v7x, 512 devices: a whole 4x8x8 slice. The times are simulated.
512 devices in a mesh: row: 16 (over z_lo, x, core), col: 32 (over y, z_hi).
Axes of the slice: x: 4, y: 8, z: 8 (z_hi: 4, z_lo: 2; z = z_hi * 2 + z_lo), core: 2. Of those that a mesh axis runs over, the one named last changes fastest.
Arguments:
- pair: bfloat16 [512, 512, 128], P('row', 'col'), may hold values from -6 to 6
- pair_mask: int32 [512, 512], P('row', 'col'), may hold values from 0 to 1, as said below
- gain_tri: float32 [128], replicated, may hold values from 0.1 to 1.9
- w_left: bfloat16 [128, 256], replicated, may hold values from -0.5 to 0.5
- w_right: bfloat16 [128, 256], replicated, may hold values from -0.5 to 0.5
- w_tri_gate: bfloat16 [128, 128], replicated, may hold values from -0.5 to 0.5
- gain_mid: float32 [128], replicated, may hold values from 0.1 to 1.9
- w_tri_out: bfloat16 [128, 128], replicated, may hold values from -0.5 to 0.5
- gain_att: float32 [128], replicated, may hold values from 0.1 to 1.9
- w_attend: bfloat16 [128, 512], replicated, may hold values from -0.5 to 0.5
- w_bias: bfloat16 [128, 4], replicated, may hold values from -2 to 2
- w_attend_out: bfloat16 [128, 128], replicated, may hold values from -0.5 to 0.5
- gain_trans: float32 [128], replicated, may hold values from 0.1 to 1.9
- w_trans_in: bfloat16 [128, 1024], replicated, may hold values from -0.5 to 0.5
- w_trans_out: bfloat16 [512, 128], replicated, may hold values from -0.25 to 0.25
Outputs:
- pair_out: bfloat16 [512, 512, 128], P('row', 'col')
Inputs may be any that keep to these rules, and one draw needn't show every extreme that they name: `pair_mask`: 1 where the pair of tokens is present and observed, else 0; tokens from some position on to the end are padding, and their rows and columns are 0.
All inputs are finite; a program needn't handle non-finite values.
Results may differ from a plain program's by a relative error of at most 0.025.
Values may be sent and summed in bfloat16 or wider, within the bound.
A program may use at most 64 MiB of HBM per device.

v0:
```python
import math

import jax
import jax.numpy as jnp
from jax import lax
from jax.sharding import PartitionSpec as P

HEADS = 4
HEAD_DIM = 32


EPS = 1e-05
MASKED = -1000000000.0


def from_root(block, axis, holder):
    block = jnp.where(lax.axis_index(axis) == holder, block, jnp.zeros_like(block))
    return lax.psum(block, axis)


def layer_norm(inputs, gain_vec):
    inputs = inputs.astype(jnp.float32)
    center = inputs - jnp.mean(inputs, -1, keepdims=True)
    spread = jnp.mean(center * center, -1, keepdims=True)
    return center * lax.rsqrt(spread + EPS) * gain_vec


def edges(normed, mask_flat, weight, channels):
    projected = jnp.dot(normed, weight, preferred_element_type=jnp.float32)
    return (mask_flat * jax.nn.sigmoid(projected[:, :channels]) * projected[:, channels:]).astype(
        jnp.bfloat16
    )


def per_device(
    pair,
    pair_mask,
    gain_tri,
    w_left,
    w_right,
    w_tri_gate,
    gain_mid,
    w_tri_out,
    gain_att,
    w_attend,
    w_bias,
    w_attend_out,
    gain_trans,
    w_trans_in,
    w_trans_out,
):
    rows_here, cols_here, channels = pair.shape
    cell_count = rows_here * cols_here
    flat_pair = pair.reshape(cell_count, channels)
    mask_flat = pair_mask.astype(jnp.float32).reshape(cell_count, 1)
    normed = layer_norm(flat_pair, gain_tri).astype(jnp.bfloat16)
    left_side = edges(normed, mask_flat, w_left, channels).reshape(rows_here, cols_here, channels)
    right_side = edges(normed, mask_flat, w_right, channels).reshape(rows_here, cols_here, channels)
    gathered = lax.all_gather(left_side, "row", axis=0, tiled=True)
    halves = []
    for which_half in range(2):
        halves.append(from_root(gathered, "col", 2 * lax.axis_index("row") + which_half))
    left_full = jnp.concatenate(halves, 1)
    triangle = jnp.einsum(
        "kic,kjc->ijc",
        left_full,
        lax.all_gather(right_side, "row", axis=0, tiled=True),
        preferred_element_type=jnp.float32,
    )
    tri_gate = jax.nn.sigmoid(jnp.dot(normed, w_tri_gate, preferred_element_type=jnp.float32))
    tri_normed = layer_norm(triangle.reshape(cell_count, channels), gain_mid).astype(jnp.bfloat16)
    tri_update = tri_gate * jnp.dot(tri_normed, w_tri_out, preferred_element_type=jnp.float32)
    pair_one = (flat_pair.astype(jnp.float32) + tri_update).astype(jnp.bfloat16)
    normed_two = layer_norm(pair_one, gain_att).astype(jnp.bfloat16)
    projected = jnp.dot(normed_two, w_attend, preferred_element_type=jnp.float32)
    queries = projected[:, :channels].astype(jnp.bfloat16).reshape(rows_here, cols_here, channels)
    key_vectors = (
        projected[:, channels : 2 * channels]
        .astype(jnp.bfloat16)
        .reshape(rows_here, cols_here, channels)
    )
    values = (
        projected[:, 2 * channels : 3 * channels]
        .astype(jnp.bfloat16)
        .reshape(rows_here, cols_here, channels)
    )
    att_gate = jax.nn.sigmoid(projected[:, 3 * channels :])
    pair_bias = jnp.dot(normed_two, w_bias, preferred_element_type=jnp.float32).astype(jnp.bfloat16)
    pair_bias = jnp.transpose(pair_bias.reshape(rows_here, cols_here, HEADS), (2, 0, 1))
    mask_bf = pair_mask.astype(jnp.bfloat16)
    score_scale = 1.0 / math.sqrt(HEAD_DIM)
    bias_gathered = lax.all_gather(pair_bias, "row", axis=1, tiled=True)
    bias_pieces = []
    for which_half in range(2):
        bias_pieces.append(from_root(bias_gathered, "col", 2 * lax.axis_index("row") + which_half))
    bias_full = jnp.concatenate(bias_pieces, 2)
    query_four = queries.reshape(rows_here, cols_here, HEADS, HEAD_DIM)
    running_max = jnp.full((HEADS, rows_here, cols_here), -1e30, jnp.float32)
    key_part = lax.all_gather(key_vectors, "row", axis=0, tiled=True)
    value_part = lax.all_gather(values, "row", axis=0, tiled=True)
    mask_part = lax.all_gather(mask_bf, "row", axis=0, tiled=True)
    key_count = key_part.shape[0]
    key_part = key_part.reshape(key_count, cols_here, HEADS, HEAD_DIM)
    value_part = value_part.reshape(key_count, cols_here, HEADS, HEAD_DIM)
    scores = (
        jnp.einsum("ijhd,kjhd->hijk", query_four, key_part, preferred_element_type=jnp.float32)
        * score_scale
    )
    bias_part = bias_full.astype(jnp.float32)
    scores = scores + jnp.transpose(bias_part, (0, 2, 1))[:, :, None, :]
    scores = jnp.where(jnp.transpose(mask_part)[None, None] > 0.5, scores, MASKED)
    new_max = jnp.maximum(running_max, jnp.max(scores, -1))
    weight = jnp.exp(scores - new_max[..., None])
    running_sum = jnp.sum(weight, -1)
    weighted = jnp.einsum(
        "hijk,kjhd->ijhd",
        weight.astype(jnp.bfloat16),
        value_part,
        preferred_element_type=jnp.float32,
    )
    running_max, running_sum, weighted = (new_max, running_sum, weighted)
    attended = (weighted / jnp.transpose(running_sum, (1, 2, 0))[..., None]).reshape(
        cell_count, channels
    )
    gated = (att_gate * attended).astype(jnp.bfloat16)
    pair_two = (
        pair_one.astype(jnp.float32)
        + jnp.dot(gated, w_attend_out, preferred_element_type=jnp.float32)
    ).astype(jnp.bfloat16)
    normed_three = layer_norm(pair_two, gain_trans).astype(jnp.bfloat16)
    expanded = jnp.dot(normed_three, w_trans_in, preferred_element_type=jnp.float32)
    trans_width = w_trans_out.shape[0]
    hidden = (jax.nn.silu(expanded[:, :trans_width]) * expanded[:, trans_width:]).astype(
        jnp.bfloat16
    )
    pair_out = (
        pair_two.astype(jnp.float32)
        + jnp.dot(hidden, w_trans_out, preferred_element_type=jnp.float32)
    ).astype(jnp.bfloat16)
    return pair_out.reshape(rows_here, cols_here, channels)


def solution(mesh):
    in_specs = (
        P("row", "col", None),
        P("row", "col"),
        P(),
        P(),
        P(),
        P(),
        P(),
        P(),
        P(),
        P(),
        P(),
        P(),
        P(),
        P(),
        P(),
    )
    out_specs = P("row", "col", None)
    return jax.shard_map(
        per_device, mesh=mesh, in_specs=in_specs, out_specs=out_specs, check_vma=False
    )
```

profile of v0, /device:TPU:1, one launch (start us, length us, event | category | flops | bytes accessed | tf_op | source)
XLA Modules:
  0.0 887.6 jit_solution(10896927593864254962)
XLA Ops:
  6.5 1.1 convert_reduce_fusion
  7.7 1.1 multiply_reduce_fusion.3
  8.8 0.1 div.53
  8.9 0.1 rsqrt.39
  9.0 1.1 fusion.52
  10.1 1.0 fusion.68
  11.1 1.0 fusion.69
  12.2 0.1 copy.57
  12.3 0.1 mul.133
  12.4 0.9 fusion.37
  13.3 0.0 all-gather.6.cloned.1.call-start
  13.3 0.7 all-gather.6.cloned.1.call-update
  14.0 0.0 all-reduce.7.cloned.1.call-start
  14.1 44.7 %all-gather.8.cloned.1.call-done = bf16[512,16,128]{2,1,0:T(8,128)(2,1)} async-done(((bf16[32,16,128]{2,1,0:T(8,128)(2,1)}), bf16[512,16,128]{2,1,0:T(8,128)(2,1)}) %all-gather.8.cloned.1.call-update) | async-done | bytes 2097168 | tf_op jit(solution)/shard_map/all_gather | solution.py:59
  58.8 3.9 copy.58
  62.7 2.3 broadcast_select_fusion.1
  65.0 0.0 all-reduce.7.cloned.1.call-update
  65.1 0.0 all-reduce.5.cloned.1.call-start
  65.1 0.7 copy-done.10
  65.8 0.2 fusion.21
  66.0 34.2 %all-gather.6.cloned.1.call-done = bf16[512,16,128]{2,1,0:T(8,128)(2,1)} async-done(((bf16[32,16,128]{2,1,0:T(8,128)(2,1)}), bf16[512,16,128]{2,1,0:T(8,128)(2,1)}) %all-gather.6.cloned.1.call-update) | async-done | bytes 2097168 | tf_op jit(solution)/shard_map/all_gather | solution.py:67
  100.2 4.8 copy.60
  105.1 318.7 %all-reduce.7.cloned.1.call-done = (bf16[512,16,128]{0,1,2:T(8,128)(2,1)}, bf16[512,16,128]{0,1,2:T(8,128)(2,1)}) async-done(((bf16[512,16,128]{0,1,2:T(8,128)(2,1)}, bf16[512,16,128]{0,1,2:T(8,128)(2,1)}), (bf16[512,16,128]{0,1,2:T(8,128)(2,1)}, bf16[512,16,128]{0,1,2:T(8,128)(2,1)})) %all-reduce.7.cloned.1.call-update) | async-done | bytes 4194320 | tf_op jit(solution)/shard_map/psum | solution.py:18
  423.8 4.1 fusion.64
  427.9 0.1 copy.62
  428.0 0.1 copy.63
  428.0 0.1 div.59
  428.1 0.5 copy.61
  428.6 0.2 multiply_reduce_fusion
  428.8 0.1 copy.64
  428.9 0.1 rsqrt.41
  429.0 0.2 fusion.49
  429.2 0.3 fusion.65
  429.5 0.2 multiply_reduce_fusion.2
  429.8 0.2 multiply_convert_fusion.1
  430.0 0.1 convolution_convert_fusion
  430.1 0.1 reshape.141
  430.3 42.4 %all_gather.23 = bf16[4,512,16]{2,1,0:T(8,128)(2,1)S(1)} all-gather(bf16[4,32,16]{2,1,0:T(8,128)(2,1)S(1)} %bitcast.76), channel_id=1, replica_groups=mesh['row'=16,'col'=32] {'row'}, dimensions={1}, use_global_device_ids=true | all-gather | bytes 69632 | tf_op jit(solution)/shard_map/all_gather | solution.py:92
  472.7 1.1 broadcast_select_fusion.3
  473.8 1.2 fusion.66
  475.0 0.0 all-reduce.5.cloned.1.call-update
  475.0 0.0 all-gather.12.cloned.1.call-start
  475.1 0.8 fusion.63
  475.9 0.0 all-gather.10.cloned.1.call-start
  475.9 0.5 all-gather.10.cloned.1.call-update
  476.4 16.6 %all-gather = bf16[16,32,16]{1,2,0:T(8,128)(2,1)S(1)} all-gather(bf16[1,32,16]{1,2,0:T(8,128)(2,1)S(1)} %get-tuple-element.18), channel_id=1, replica_groups=mesh['row'=16,'col'=32] {'row'}, dimensions={0}, use_global_device_ids=true | all-gather | bytes 17408 | tf_op jit(solution)/shard_map/all_gather | solution.py:101
  493.1 0.1 reshape.148
  493.2 0.2 reshape_reshape.3
  493.5 273.7 %all-reduce.5.cloned.1.call-done = (bf16[4,512,16]{2,1,0:T(8,128)(2,1)}, bf16[4,512,16]{2,1,0:T(8,128)(2,1)}) async-done(((bf16[4,512,16]{2,1,0:T(8,128)(2,1)}, bf16[4,512,16]{2,1,0:T(8,128)(2,1)}), (bf16[4,512,16]{2,1,0:T(8,128)(2,1)}, bf16[4,512,16]{2,1,0:T(8,128)(2,1)})) %all-reduce.5.cloned.1.call-update) | async-done | bytes 131088 | tf_op jit(solution)/shard_map/psum | solution.py:18
  767.2 1.2 copy.70
  768.4 1.2 copy.71
  769.6 56.1 %all-gather.12.cloned.1.call-done = bf16[512,16,128]{2,1,0:T(8,128)(2,1)} async-done(((bf16[32,16,128]{2,1,0:T(8,128)(2,1)}), bf16[512,16,128]{2,1,0:T(8,128)(2,1)}) %all-gather.12.cloned.1.call-update) | async-done | bytes 2097168 | tf_op jit(solution)/shard_map/all_gather | solution.py:99
  825.8 3.0 copy.67
  828.8 1.4 fusion.7
  830.2 1.6 fusion.5
  831.9 35.4 %all-gather.10.cloned.1.call-done = bf16[512,16,128]{2,1,0:T(8,128)(2,1)} async-done(((bf16[32,16,128]{2,1,0:T(8,128)(2,1)}), bf16[512,16,128]{2,1,0:T(8,128)(2,1)}) %all-gather.10.cloned.1.call-update) | async-done | bytes 2097168 | tf_op jit(solution)/shard_map/all_gather | solution.py:100
  867.2 4.3 copy.65
  871.6 3.2 fusion.27
  874.8 2.3 copy.74
  877.1 0.5 reshape.142
  877.6 1.3 fusion.67
  878.9 0.2 multiply_reduce_fusion.1
  879.2 0.5 fusion.55
  879.7 1.1 fusion.26
  (40 shorter events, 0.2 us)
Async XLA Ops:
  6.5 872.7 %copy-start = (bf16[128,1024]{1,0:T(8,128)(2,1)S(1)}, bf16[128,1024]{1,0:T(8,128)(2,1)}, u32[]{:S(2)}) copy-start(bf16[128,1024]{1,0:T(8,128)(2,1)} %param.28) | copy-start | bytes 786436
  6.5 5.7 copy-start.4
  6.5 52.3 %all-gather.8.cloned.1.call-start = ((), (), s32[]{:S(2)}) async-start(), calls=%async_computation.1 | async-start | bytes 2228224 | tf_op jit(solution)/shard_map/all_gather | solution.py:59
  13.3 86.9 %all-gather.6.cloned.1.call-start = ((), (), s32[]{:S(2)}) async-start(), calls=%async_computation | async-start | bytes 2228224 | tf_op jit(solution)/shard_map/all_gather | solution.py:67
  14.0 409.8 %all-reduce.7.cloned.1.call-start = ((), (), s32[]{:S(2)}) async-start(), calls=%async_computation.5 | async-start | bytes 8388608 | tf_op jit(solution)/shard_map/psum | solution.py:18
  65.0 0.8 copy-start.10
  65.1 702.1 %all-reduce.5.cloned.1.call-start = ((), (), s32[]{:S(2)}) async-start(), calls=%async_computation.4 | async-start | bytes 2097152 | tf_op jit(solution)/shard_map/psum | solution.py:18
  427.9 1.1 copy-start.6
  427.9 1.3 copy-start.1
  427.9 1.3 copy-start.3
  427.9 1.9 copy-start.7
  428.1 1.9 copy-start.5
  429.0 44.8 %copy-start.2 = (bf16[128,512]{1,0:T(8,128)(2,1)S(1)}, bf16[128,512]{1,0:T(8,128)(2,1)}, u32[]{:S(2)}) copy-start(bf16[128,512]{1,0:T(8,128)(2,1)} %param.24) | copy-start | bytes 393220
  475.0 350.7 %all-gather.12.cloned.1.call-start = ((), (), s32[]{:S(2)}) async-start(), calls=%async_computation.3 | async-start | bytes 2228224 | tf_op jit(solution)/shard_map/all_gather | solution.py:99
  475.9 391.4 %all-gather.10.cloned.1.call-start = ((), (), s32[]{:S(2)}) async-start(), calls=%async_computation.2 | async-start | bytes 2228224 | tf_op jit(solution)/shard_map/all_gather | solution.py:100
  874.8 2.8 copy-start.11
  874.8 4.4 copy-start.8
  877.6 2.1 copy-start.9
Sparse Core Ops, SparseCore 0:
  13.4 45.3 all-gather.7
  61.0 39.2 all-gather.5
  103.2 320.5 all-reduce.6
  475.2 291.9 all-reduce.4
  769.4 56.3 all-gather.11
  828.0 39.2 all-gather.9
where the time goes:
time: 888 us
  waiting for transfers between devices  764 us (86%)
  blocking collectives  59 us (7%)
  local copies, waits for them, and re-layouts  24.5 us (3%)
  matrix products  15.6 us (2%)
  between operations  13.8 us (2%)
  other arithmetic  10.4 us (1%)
    psum x2, waiting for transfers between devices, from_root(): return lax.psum(block, axis)  592 us
    all_gather x1, waiting for transfers between devices, per_device(): key_part = lax.all_gather(key_vectors, 'row', axis=0, tiled=True)  56.1 us
    all_gather x1, waiting for transfers between devices, per_device(): gathered = lax.all_gather(left_side, 'row', axis=0, tiled=True)  44.7 us
    all_gather x1, blocking collectives, per_device(): bias_gathered = lax.all_gather(pair_bias, 'row', axis=1, tiled=True)  42.4 us
    all_gather x1, waiting for transfers between devices, per_device(): value_part = lax.all_gather(values, 'row', axis=0, tiled=True)  35.4 us
    all_gather x1, waiting for transfers between devices, per_device(): lax.all_gather(right_side, 'row', axis=0, tiled=True)  34.2 us
  transfers between devices with their start and end apart: 6, of which 6 were waited for; matrix products, arithmetic and copies ran while one was open for 2% of the time, Pallas kernels for 0%

commit v1 on v0

v1 whole, which is shorter than its diff:
```python
import math

import jax
import jax.numpy as jnp
from jax import lax
from jax.sharding import PartitionSpec as P

HEADS = 4
HEAD_DIM = 32


EPS = 1e-05
MASKED = -1000000000.0
ROWS = 16
BY_ZH = [[y * 4 + z for z in range(4)] for y in range(8)]
BY_Y = [[y * 4 + z for y in range(8)] for z in range(4)]


def layer_norm(inputs, gain_vec):
    inputs = inputs.astype(jnp.float32)
    center = inputs - jnp.mean(inputs, -1, keepdims=True)
    spread = jnp.mean(center * center, -1, keepdims=True)
    return center * lax.rsqrt(spread + EPS) * gain_vec


def edges(normed, mask_flat, weight, channels):
    projected = jnp.dot(normed, weight, preferred_element_type=jnp.float32)
    return (mask_flat * jax.nn.sigmoid(projected[:, :channels]) * projected[:, channels:]).astype(
        jnp.bfloat16
    )


def per_device(
    pair,
    pair_mask,
    gain_tri,
    w_left,
    w_right,
    w_tri_gate,
    gain_mid,
    w_tri_out,
    gain_att,
    w_attend,
    w_bias,
    w_attend_out,
    gain_trans,
    w_trans_in,
    w_trans_out,
):
    rows_here, cols_here, channels = pair.shape
    cell_count = rows_here * cols_here
    flat_pair = pair.reshape(cell_count, channels)
    mask_flat = pair_mask.astype(jnp.float32).reshape(cell_count, 1)
    normed = layer_norm(flat_pair, gain_tri).astype(jnp.bfloat16)
    left_side = edges(normed, mask_flat, w_left, channels).reshape(rows_here, cols_here, channels)
    right_side = edges(normed, mask_flat, w_right, channels).reshape(rows_here, cols_here, channels)
    groups = channels // ROWS
    both = jnp.stack([left_side, right_side])
    both = both.reshape(2, rows_here, cols_here, ROWS, groups)
    both = jnp.transpose(both, (3, 0, 4, 1, 2))
    both = lax.all_to_all(both, "row", 0, 0)
    both = jnp.transpose(both, (1, 2, 4, 0, 3)).reshape(2, groups, cols_here, ROWS * rows_here)
    left_here = lax.all_gather(both[0], "col", axis=1, tiled=True, axis_index_groups=BY_ZH)
    right_here = lax.all_gather(both[1], "col", axis=1, tiled=True, axis_index_groups=BY_Y)
    part = jnp.einsum("cik,cjk->cij", left_here, right_here, preferred_element_type=jnp.float32)
    part = part.astype(jnp.bfloat16).reshape(groups, 64, 8, cols_here)
    part = jnp.transpose(part, (2, 0, 1, 3))
    part = lax.all_to_all(part, "col", 0, 0, axis_index_groups=BY_Y)
    part = part.reshape(8, groups, 2, rows_here, cols_here)
    part = jnp.transpose(part, (0, 2, 1, 3, 4)).reshape(ROWS, groups, rows_here, cols_here)
    part = lax.all_to_all(part, "row", 0, 0)
    triangle = jnp.transpose(part.astype(jnp.float32), (2, 3, 0, 1))
    tri_gate = jax.nn.sigmoid(jnp.dot(normed, w_tri_gate, preferred_element_type=jnp.float32))
    tri_normed = layer_norm(triangle.reshape(cell_count, channels), gain_mid).astype(jnp.bfloat16)
    tri_update = tri_gate * jnp.dot(tri_normed, w_tri_out, preferred_element_type=jnp.float32)
    pair_one = (flat_pair.astype(jnp.float32) + tri_update).astype(jnp.bfloat16)
    normed_two = layer_norm(pair_one, gain_att).astype(jnp.bfloat16)
    projected = jnp.dot(normed_two, w_attend, preferred_element_type=jnp.float32)
    att_gate = jax.nn.sigmoid(projected[:, 3 * channels :])
    pair_bias = jnp.dot(normed_two, w_bias, preferred_element_type=jnp.float32).astype(jnp.bfloat16)
    qkv = projected[:, : 3 * channels].astype(jnp.bfloat16)
    qkv = qkv.reshape(rows_here, 4, cols_here // 4, 3, HEADS, HEAD_DIM)
    qkv = jnp.transpose(qkv, (4, 1, 3, 5, 2, 0)).reshape(ROWS, 3 * HEAD_DIM * 128)
    bias_send = jnp.transpose(pair_bias.reshape(rows_here, cols_here, HEADS), (2, 1, 0))
    bias_send = jnp.broadcast_to(bias_send.reshape(HEADS, 1, 512), (HEADS, 4, 512)).reshape(ROWS, 512)
    mask_send = jnp.transpose(pair_mask.astype(jnp.bfloat16).reshape(rows_here, 4, 4), (1, 2, 0))
    mask_send = jnp.broadcast_to(mask_send.reshape(1, 4, 128), (HEADS, 4, 128)).reshape(ROWS, 128)
    message = jnp.concatenate([qkv, bias_send, mask_send], 1)
    message = lax.all_to_all(message, "row", 0, 0)
    width = 3 * HEAD_DIM * 128
    qkv = message[:, :width].reshape(ROWS, 3, HEAD_DIM, 4, rows_here)
    qkv = jnp.transpose(qkv, (1, 3, 2, 0, 4)).reshape(3, 4, HEAD_DIM, 512)
    bias = message[:, width : width + 512].reshape(ROWS, cols_here, rows_here)
    bias = jnp.transpose(bias, (1, 0, 2)).reshape(cols_here, 512)
    bias = lax.all_gather(bias, "col", axis=0, tiled=True)
    mask = message[:, width + 512 :].reshape(ROWS, 4, rows_here)
    mask = jnp.transpose(mask, (1, 0, 2)).reshape(4, 1, 512)
    scores = jnp.einsum("jdi,jdk->jik", qkv[0], qkv[1], preferred_element_type=jnp.float32)
    scores = scores * (1.0 / math.sqrt(HEAD_DIM)) + bias.astype(jnp.float32)[None]
    scores = jnp.where(mask > 0.5, scores, MASKED)
    weight = jnp.exp(scores - jnp.max(scores, -1, keepdims=True))
    total = jnp.sum(weight, -1)
    weighted = jnp.einsum(
        "jdk,jik->jdi", qkv[2], weight.astype(jnp.bfloat16), preferred_element_type=jnp.float32
    )
    attended = (weighted / total[:, None, :]).astype(jnp.bfloat16)
    attended = attended.reshape(4, HEAD_DIM, ROWS, rows_here)
    attended = jnp.transpose(attended, (2, 0, 1, 3))
    attended = lax.all_to_all(attended, "row", 0, 0)
    attended = attended.reshape(HEADS, 4, 4, HEAD_DIM, rows_here)
    attended = jnp.transpose(attended, (4, 1, 2, 0, 3)).reshape(cell_count, channels)
    attended = attended.astype(jnp.float32)
    gated = (att_gate * attended).astype(jnp.bfloat16)
    pair_two = (
        pair_one.astype(jnp.float32)
        + jnp.dot(gated, w_attend_out, preferred_element_type=jnp.float32)
    ).astype(jnp.bfloat16)
    normed_three = layer_norm(pair_two, gain_trans).astype(jnp.bfloat16)
    expanded = jnp.dot(normed_three, w_trans_in, preferred_element_type=jnp.float32)
    trans_width = w_trans_out.shape[0]
    hidden = (jax.nn.silu(expanded[:, :trans_width]) * expanded[:, trans_width:]).astype(
        jnp.bfloat16
    )
    pair_out = (
        pair_two.astype(jnp.float32)
        + jnp.dot(hidden, w_trans_out, preferred_element_type=jnp.float32)
    ).astype(jnp.bfloat16)
    return pair_out.reshape(rows_here, cols_here, channels)


def solution(mesh):
    in_specs = (
        P("row", "col", None),
        P("row", "col"),
        P(),
        P(),
        P(),
        P(),
        P(),
        P(),
        P(),
        P(),
        P(),
        P(),
        P(),
        P(),
        P(),
    )
    out_specs = P("row", "col", None)
    return jax.shard_map(
        per_device, mesh=mesh, in_specs=in_specs, out_specs=out_specs, check_vma=False
    )
```

time: 888 us -> 254 us (0.29)
  waiting for transfers between devices: 764 us -> 24.2 us
  blocking collectives: 59 us -> 149 us
  starting transfers between devices: 0.21 us -> 11.7 us
    psum x2 -> x0, waiting for transfers between devices: 592 us -> none  [from_root(): return lax.psum(block, axis)]
    all_gather x4 -> x1, waiting for transfers between devices: 170 us -> 19.1 us  [per_device(): lax.all_gather(both[1], 'col', axis=1, tiled=True, axis_index_groups=BY_Y)]
    all_to_all x0 -> x4, blocking collectives: none -> 63.4 us  [the longest x1 23.5 us: per_device(): attended = lax.all_to_all(attended, 'row', 0, 0)]
    all_gather x2, blocking collectives: 59 us -> 85.8 us  [the longest x1 68.6 us: per_device(): bias = lax.all_gather(bias, 'col', axis=0, tiled=True)]
    all_gather x4 -> x0, local copies, waits for them, and re-layouts: 16.1 us -> none  [the longest x1 4.85 us: per_device(): lax.all_gather(right_side, 'row', axis=0, tiled=True)]
    all_to_all x0 -> x1, starting transfers between devices: none -> 11.7 us  [per_device(): part = lax.all_to_all(part, 'row', 0, 0)]
  transfers between devices with their start and end apart: 6 -> 2, of which waited for: 6 -> 2; matrix products, arithmetic and copies ran while one was open for 2% -> 1% of each run, Pallas kernels for 0% -> 0%
where the time goes in v1:
time: 254 us; the launch traced here: 253 us
  blocking collectives  149 us (59%)
  local copies, waits for them, and re-layouts  31 us (12%)
  waiting for transfers between devices  24.2 us (10%)
  between operations  14 us (6%)
  matrix products  12.7 us (5%)
  starting transfers between devices  11.7 us (5%)
  other arithmetic  10.2 us (4%)
    all_gather x1, blocking collectives, per_device(): bias = lax.all_gather(bias, 'col', axis=0, tiled=True)  68.6 us
    all_to_all x1, blocking collectives, per_device(): attended = lax.all_to_all(attended, 'row', 0, 0)  23.5 us
    all_gather x1, waiting for transfers between devices, per_device(): lax.all_gather(both[1], 'col', axis=1, tiled=True, axis_index_groups=BY_Y)  19.1 us
    all_gather x1, blocking collectives, per_device(): lax.all_gather(both[0], 'col', axis=1, tiled=True, axis_index_groups=BY_ZH)  17.2 us
    all_to_all x1, blocking collectives, per_device(): both = lax.all_to_all(both, 'row', 0, 0)  16.5 us
    all_to_all x1, blocking collectives, per_device(): message = lax.all_to_all(message, 'row', 0, 0)  11.8 us
    all_to_all x1, starting transfers between devices, per_device(): part = lax.all_to_all(part, 'row', 0, 0)  11.7 us
    all_to_all x1, blocking collectives, per_device(): part = lax.all_to_all(part, 'col', 0, 0, axis_index_groups=BY_Y)  11.6 us
  transfers between devices with their start and end apart: 2, of which 2 were waited for; matrix products, arithmetic and copies ran while one was open for 1% of the time, Pallas kernels for 0%

profile of v1, /device:TPU:1, one launch (start us, length us, event | category | flops | bytes accessed | tf_op | source)
XLA Modules:
  0.0 253.0 jit_solution(8883573177476471247)
XLA Ops:
  6.5 1.1 convert_reduce_fusion
  7.7 1.1 multiply_reduce_fusion.3
  8.9 0.8 fusion.58
  9.9 1.1 fusion.40
  11.0 1.0 fusion.62
  12.1 1.0 fusion.61
  13.6 0.8 stack.8
  14.4 1.8 stack.7
  16.2 1.7 maximum_bitcast_fusion
  17.9 1.0 copy.111
  18.9 1.0 reshape.202
  19.9 16.5 %all_to_all.32 = bf16[16,2,4096]{2,1,0:T(2,128)(2,1)S(1)} all-to-all(bf16[16,2,4096]{2,1,0:T(2,128)(2,1)S(1)} %reshape.202), channel_id=1, replica_groups=mesh['row'=16,'col'=32] {'row'}, dimensions={0} | all-to-all | bytes 524288 | tf_op jit(solution)/shard_map/all_to_all | solution.py:61
  36.4 0.5 reshape.203
  36.9 0.3 bitcast_bitcast_fusion
  37.2 0.3 fusion.56
  37.5 0.3 copy.113
  37.8 1.1 squeeze.16
  39.0 0.3 copy.112
  39.3 0.4 squeeze.15
  39.8 17.2 %all_gather.9 = bf16[8,64,512]{2,1,0:T(8,128)(2,1)S(1)} all-gather(bf16[8,16,512]{2,1,0:T(8,128)(2,1)S(1)} %squeeze.15), channel_id=1, replica_groups={{0,1,2,3},{4,5,6,7},{8,9,10,11},{12,13,14,15},{16,17,18,19},{20,21,22,2..., dimensions={1}, use_global_device_ids=true | all-gather | bytes 655360 | tf_op jit(solution)/shard_map/all_gather | solution.py:63
  57.0 19.1 %all-gather.2.cloned.1.call-done = bf16[8,128,512]{2,1,0:T(8,128)(2,1)} async-done(((bf16[8,16,512]{2,1,0:T(8,128)(2,1)}), bf16[8,128,512]{2,1,0:T(8,128)(2,1)}) %all-gather.2.cloned.1.call-update) | async-done | bytes 1048592 | tf_op jit(solution)/shard_map/all_gather | solution.py:64
  76.1 1.7 convolution_convert_fusion
  78.3 11.6 %all_to_all.33 = bf16[8,2,4096]{2,1,0:T(2,128)(2,1)S(1)} all-to-all(bf16[8,2,4096]{2,1,0:T(2,128)(2,1)S(1)} %reshape.204), channel_id=1, replica_groups={{0,4,8,12,16,20,24,28},{1,5,9,13,17,21,25,29},{2,6,10,14,18,22,26,30},{..., dimensions={0} | all-to-all | bytes 262144 | tf_op jit(solution)/shard_map/all_to_all | solution.py:68
  90.3 1.2 reshape.206
  91.5 11.7 %all-to-all-start.2 = ((bf16[16,2,2048]{2,1,0:T(2,128)(2,1)}), bf16[16,2,2048]{2,1,0:T(2,128)(2,1)S(1)}, u32[]{:S(2)}, u32[]{:S(2)}) async-start(bf16[16,2,2048]{2,1,0:T(2,128)(2,1)} %reshape.206), calls=%async_computation.2 | async-start | bytes 262144 | tf_op jit(solution)/shard_map/all_to_all | solution.py:71
  103.3 0.9 fusion.9
  104.2 5.1 %all-to-all-done.2 = bf16[16,2,2048]{2,1,0:T(2,128)(2,1)S(1)} async-done(((bf16[16,2,2048]{2,1,0:T(2,128)(2,1)}), bf16[16,2,2048]{2,1,0:T(2,128)(2,1)S(1)}, u32[]{:S(2)}, u32[]{:S(2)}) %all-to-all-start.2) | async-done | bytes 131104 | tf_op jit(solution)/shard_map/all_to_all | solution.py:71
  109.3 0.3 reshape.207
  110.5 0.6 copy.116
  111.2 1.6 reshape.187
  112.7 1.4 fusion.59
  114.4 0.4 copy-done.1
  114.8 0.9 multiply_convert_fusion.1
  116.2 1.3 fusion.63
  117.4 1.2 slice.144
  118.6 0.9 reshape.188
  119.5 1.8 copy.120
  121.4 1.6 reshape.189
  123.1 0.5 broadcast.143
  123.6 0.8 reduce.4
  124.4 0.5 reshape.208
  124.9 11.8 %all_to_all.34 = bf16[16,2,6464]{2,1,0:T(2,128)(2,1)S(1)} all-to-all(bf16[16,2,6464]{2,1,0:T(2,128)(2,1)S(1)} %reshape.208), channel_id=1, replica_groups=mesh['row'=16,'col'=32] {'row'}, dimensions={0} | all-to-all | bytes 827392 | tf_op jit(solution)/shard_map/all_to_all | solution.py:89
  136.7 0.7 reshape.209
  137.9 68.6 %all_gather.11 = bf16[512,512]{1,0:T(8,128)(2,1)S(1)} all-gather(bf16[16,512]{1,0:T(8,128)(2,1)S(1)} %reshape.196), channel_id=1, replica_groups=mesh['row'=16,'col'=32] {'col'}, dimensions={0}, use_global_device_ids=true | all-gather | bytes 540672 | tf_op jit(solution)/shard_map/all_gather | solution.py:95
  206.7 1.3 reshape.194
  208.0 1.5 fusion.55
  209.5 0.3 copy.126
  209.8 0.4 squeeze.19
  210.3 1.4 copy.125
  211.7 0.4 squeeze.18
  212.1 0.3 copy.123
  212.5 0.4 squeeze.17
  212.9 1.1 fusion.2
  214.1 1.2 fusion
  215.3 1.3 fusion.18
  216.6 0.3 reshape.197
  217.0 0.5 reshape.210
  217.5 23.5 %all_to_all.35 = bf16[16,2,2048]{2,1,0:T(2,128)(2,1)S(1)} all-to-all(bf16[16,2,2048]{2,1,0:T(2,128)(2,1)S(1)} %reshape.210), channel_id=1, replica_groups=mesh['row'=16,'col'=32] {'row'}, dimensions={0} | all-to-all | bytes 262144 | tf_op jit(solution)/shard_map/all_to_all | solution.py:109
  241.0 0.3 reshape.211
  241.4 1.1 copy.131
  242.5 0.5 reshape.200
  243.0 1.2 fusion.60
  244.6 0.5 fusion.43
  245.1 1.1 fusion.14
  (74 shorter events, 4.6 us)
Async XLA Ops:
  6.5 238.0 %copy-start = (bf16[128,1024]{1,0:T(8,128)(2,1)S(1)}, bf16[128,1024]{1,0:T(8,128)(2,1)}, u32[]{:S(2)}) copy-start(bf16[128,1024]{1,0:T(8,128)(2,1)} %param.28) | copy-start | bytes 786436
  6.5 69.6 %all-gather.2.cloned.1.call-start = ((), (), s32[]{:S(2)}) async-start(), calls=%async_computation.5 | async-start | bytes 1179648 | tf_op jit(solution)/shard_map/all_gather | solution.py:64
  39.3 63.9 %copy-start.8 = (bf16[128,128]{1,0:T(8,128)(2,1)S(1)}, bf16[128,128]{1,0:T(8,128)(2,1)}, u32[]{:S(2)}) copy-start(bf16[128,128]{1,0:T(8,128)(2,1)} %param.20) | copy-start | bytes 98308
  91.5 17.8 %all-to-all-start.2 = ((bf16[16,2,2048]{2,1,0:T(2,128)(2,1)}), bf16[16,2,2048]{2,1,0:T(2,128)(2,1)S(1)}, u32[]{:S(2)}, u32[]{:S(2)}) async-start(bf16[16,2,2048]{2,1,0:T(2,128)(2,1)} %reshape.206), calls=%async_computation.2 | async-start | bytes 262144 | tf_op jit(solution)/shard_map/all_to_all | solution.py:71
  109.6 3.1 %copy-start.3 = (bf16[32,16,128]{2,1,0:T(8,128)(2,1)S(1)}, bf16[32,16,128]{2,1,0:T(8,128)(2,1)}, u32[]{:S(2)}) copy-start(bf16[32,16,128]{2,1,0:T(8,128)(2,1)} %param.15) | copy-start | bytes 393220
  110.1 5.6 %copy-start.5 = (bf16[128,4]{0,1:T(4,128)(2,1)S(1)}, bf16[128,4]{0,1:T(4,128)(2,1)}, u32[]{:S(2)}) copy-start(bf16[128,4]{0,1:T(4,128)(2,1)} %param.25) | copy-start | bytes 3076
  111.1 5.0 %copy-start.4 = (bf16[128,512]{1,0:T(8,128)(2,1)S(1)}, bf16[128,512]{1,0:T(8,128)(2,1)}, u32[]{:S(2)}) copy-start(bf16[128,512]{1,0:T(8,128)(2,1)} %param.24) | copy-start | bytes 393220
  114.1 0.7 copy-start.1
  216.5 26.5 %copy-start.2 = (f32[512,128]{1,0:T(8,128)S(1)}, f32[512,128]{1,0:T(8,128)}, u32[]{:S(2)}) copy-start(f32[512,128]{1,0:T(8,128)} %copy-done.1) | copy-start | bytes 786436
  216.6 26.5 %copy-start.9 = (bf16[128,128]{1,0:T(8,128)(2,1)S(1)}, bf16[128,128]{1,0:T(8,128)(2,1)}, u32[]{:S(2)}) copy-start(bf16[128,128]{1,0:T(8,128)(2,1)} %param.26) | copy-start | bytes 98308
  217.0 27.5 %copy-start.6 = (f32[128]{0:T(128)S(1)}, f32[128]{0:T(128)}, u32[]{:S(2)}) copy-start(f32[128]{0:T(128)} %param.27) | copy-start | bytes 1540
  241.4 3.6 %copy-start.7 = (bf16[512,128]{1,0:T(8,128)(2,1)S(1)}, bf16[512,128]{1,0:T(8,128)(2,1)}, u32[]{:S(2)}) copy-start(bf16[512,128]{1,0:T(8,128)(2,1)} %param.29) | copy-start | bytes 393220
Sparse Core Ops, SparseCore 0:
  39.1 36.9 all-gather.1

commit v2 on v1

v2 whole, which is shorter than its diff:
```python
import functools
import math

import jax
import jax.numpy as jnp
from jax import lax
from jax.experimental import pallas as pl
from jax.experimental.pallas import tpu as pltpu
from jax.sharding import PartitionSpec as P

HEADS = 4
HEAD_DIM = 32
EPS = 1e-05
MASKED = -1000000000.0
LOG2E = math.log2(math.e)
ROWS = 16
YS = 8
ZS = 4
VMEM_LIMIT = 63 * 1024 * 1024
MESH = pl.DeviceIdType.MESH
F32 = jnp.float32
BF16 = jnp.bfloat16


def dot(lhs, rhs, lhs_dim, rhs_dim):
    return lax.dot_general(
        lhs, rhs, (((lhs_dim,), (rhs_dim,)), ((), ())), preferred_element_type=F32
    )


def layer_norm(inputs, gain_vec, axis=-1):
    center = inputs - jnp.mean(inputs, axis, keepdims=True)
    spread = jnp.mean(center * center, axis, keepdims=True)
    return center * lax.rsqrt(spread + EPS) * gain_vec


def swap_blocks(arrays, width):
    arrays = list(arrays)
    lane = lax.broadcasted_iota(jnp.int32, arrays[0].shape, 1)
    step = 1
    while step < len(arrays):
        shift = width * step
        odd = (lane & shift) != 0
        fresh = list(arrays)
        for low in range(len(arrays)):
            if low & step == 0:
                high = low | step
                fresh[low] = jnp.where(odd, pltpu.roll(arrays[high], shift, 1), arrays[low])
                fresh[high] = jnp.where(odd, arrays[high], pltpu.roll(arrays[low], 128 - shift, 1))
        arrays = fresh
        step *= 2
    return arrays


def kernel(
    pair_hbm, mask_hbm, gain_tri_hbm, w_left_hbm, w_right_hbm, w_tri_gate_hbm, gain_mid_hbm,
    w_tri_out_hbm, gain_att_hbm, w_attend_hbm, w_bias_hbm, w_attend_out_hbm, gain_trans_hbm,
    w_trans_in_hbm, w_trans_out_hbm,
    out_ref,
    pair_ref, mask_ref, gain_tri, w_left, w_right, w_tri_gate, gain_mid, w_tri_out, gain_att,
    w_attend, w_bias, w_attend_out, gain_trans, w_trans_in, w_trans_out, load_sems,
    work, edge_send, edge_recv, edge_work, left_all, right_all, gate_tri, tri_work, tri_send,
    tri_recv, bias_send, bias_recv, bias_work, bias_all, bias_full, mask_cols, pair_one_t, gate_att,
    qkv_send, qkv_recv, query_buf, key_buf, value_buf, att_send, att_recv,
    edge_ss, edge_rs, left_ss, left_rs, right_ss, right_rs, tri_ss, tri_rs, bias_ss, bias_rs,
    biasz_ss, biasz_rs, biasy_ss, biasy_rs, qkv_ss, qkv_rs, att_ss, att_rs,
):
    r = lax.axis_index("row")
    c = lax.axis_index("col")
    y = c // ZS
    z = c % ZS
    up = ((y + 1) % YS) * ZS + z
    down = ((y + YS - 1) % YS) * ZS + z

    def send(src, dst, ssem, rsem, row, col):
        pltpu.make_async_remote_copy(
            src_ref=src, dst_ref=dst, send_sem=ssem, recv_sem=rsem,
            device_id=(row, col), device_id_type=MESH,
        ).start()

    def wait(ref, sem):
        pltpu.make_async_copy(ref, ref, sem).wait()

    loads = [
        pltpu.make_async_copy(src, dst, load_sems.at[at])
        for at, (src, dst) in enumerate(
            [
                (pair_hbm, pair_ref), (gain_tri_hbm, gain_tri), (mask_hbm, mask_ref),
                (w_left_hbm, w_left), (w_right_hbm, w_right), (w_tri_gate_hbm, w_tri_gate),
                (gain_mid_hbm, gain_mid), (w_tri_out_hbm, w_tri_out), (gain_att_hbm, gain_att),
                (w_bias_hbm, w_bias), (w_attend_hbm, w_attend), (w_attend_out_hbm, w_attend_out),
                (gain_trans_hbm, gain_trans), (w_trans_in_hbm, w_trans_in),
                (w_trans_out_hbm, w_trans_out),
            ]
        )
    ]
    for load in loads:
        load.start()

    barrier = pltpu.get_barrier_semaphore()

    def hello(row, col):
        pl.semaphore_signal(barrier, inc=1, device_id=(row, col), device_id_type=MESH)

    @pl.loop(1, ROWS)
    def _(s):
        hello((r + s) % ROWS, c)

    @pl.loop(1, ZS)
    def _(s):
        hello(r, y * ZS + (z + s) % ZS)

    hello(r, up)
    hello(r, down)

    @pl.loop(0, 2 * YS)
    def _(s):
        row, yy = 2 * y + s // YS, s % YS

        @pl.when(jnp.logical_or(row != r, yy != y))
        def _():
            hello(row, yy * ZS + z)

    @pl.loop(0, ROWS)
    def _(s):
        @pl.when(jnp.logical_or(s != r, r // 2 != y))
        def _():
            hello(s, (r // 2) * ZS + z)

    for load in loads[:5]:
        load.wait()
    pair = pair_ref[...].astype(F32).reshape(512, 128)
    normed = layer_norm(pair, gain_tri[...]).astype(BF16)
    work[...] = normed.astype(F32)
    normed_t = jnp.concatenate([work[pl.ds(j, 32, stride=16), :] for j in range(16)], 0).astype(BF16)
    lane = lax.broadcasted_iota(jnp.int32, (32, 512), 1)
    spread = lax.broadcasted_iota(jnp.int32, (32, 512), 0) == (lane & 31)
    mask = dot(mask_ref[...].astype(F32).astype(BF16), spread.astype(F32).astype(BF16), 1, 0)
    lane = lax.broadcasted_iota(jnp.int32, (16, 512), 1)
    own = lax.broadcasted_iota(jnp.int32, (16, 512), 0) == (lane >> 5)
    mask = jnp.sum(jnp.where(own, mask, 0.0), 0, keepdims=True)
    sides = []
    for weight in (w_left, w_right):
        projected = dot(weight[...], normed_t, 0, 1)
        sides.append((mask * jax.nn.sigmoid(projected[:128]) * projected[128:]).reshape(ROWS, 8, 512))
    edge_send[...] = jnp.concatenate(sides, 1).astype(BF16)
    edge_recv[r] = edge_send[r]

    pl.semaphore_wait(
        barrier,
        (ROWS - 1) + (ZS - 1) + 2 + 2 * (2 * YS) - jnp.where(r // 2 == y, 2, 0),
    )

    @pl.loop(1, ROWS)
    def _(s):
        to = (r + s) % ROWS
        send(edge_send.at[to], edge_recv.at[r], edge_ss.at[to], edge_rs.at[r], to, c)

    for load in loads[5:]:
        load.wait()
    gate_tri[...] = jax.nn.sigmoid(dot(normed, w_tri_gate[...], 1, 0))

    @pl.loop(1, ROWS)
    def _(s):
        of = (r + s) % ROWS
        wait(edge_recv.at[of], edge_rs.at[of])

    for v in range(4):
        pieces = [
            jnp.concatenate(
                [edge_recv[4 * a + b, :, 128 * v : 128 * v + 128].astype(F32) for a in range(4)], 0
            )
            for b in range(4)
        ]
        for q, piece in enumerate(swap_blocks(pieces, 32)):
            for a in range(4):
                edge_work.at[a][pl.ds(4 * v + q, 16, stride=16), :] = piece[16 * a : 16 * a + 16]
    for a in range(4):
        block = edge_work[a].astype(BF16).reshape(2, 8, 16, 128)
        left_all[z, :, :, 128 * a : 128 * a + 128] = block[0]
        right_all[y, :, :, 128 * a : 128 * a + 128] = block[1]

    class Ring:
        def __init__(self, buf, ss, rs, size, me, to):
            self.buf, self.ss, self.rs, self.size, self.me, self.to = buf, ss, rs, size, me, to
            self.half = buf.shape[1] // 2

        def part(self, block, chunk):
            return self.buf.at[block % self.size, pl.ds(chunk * self.half, self.half)]

        def send(self, step, chunk, way):
            block = self.me + self.size - step + 1 if way == 0 else self.me + step - 1
            part = self.part(block, chunk)
            row, col = self.to[way]
            send(part, part, self.ss.at[way, step, chunk], self.rs.at[way, step, chunk], row, col)

        def land(self, step, chunk, way):
            block = self.me + self.size - step if way == 0 else self.me + step
            wait(self.part(block, chunk), self.rs.at[way, step, chunk])

        def start(self):
            for chunk in range(2):
                for way in range(2):
                    self.send(1, chunk, way)

        def turn(self, step, chunks=(0, 1)):
            last = self.size // 2
            for chunk in chunks:
                for way in range(2):
                    if step == last and way != chunk:
                        continue
                    self.land(step, chunk, way)
                    if step < last - 1 or (step == last - 1 and way == chunk):
                        self.send(step + 1, chunk, way)

        def sent(self):
            for step in range(1, self.size // 2 + 1):
                for chunk in range(2):
                    for way in range(2):
                        if step < self.size // 2 or way == chunk:
                            wait(self.part(0, 0), self.ss.at[way, step, chunk])

    y_ring = ((r, up), (r, down))
    rights_ring = Ring(right_all, right_ss, right_rs, YS, y, y_ring)
    lefts_ring = Ring(
        left_all, left_ss, left_rs, ZS, z,
        ((r, y * ZS + (z + 1) % ZS), (r, y * ZS + (z + ZS - 1) % ZS)),
    )
    bias_ring = Ring(bias_all, biasy_ss, biasy_rs, YS, y, y_ring)
    rights_ring.start()
    lefts_ring.start()
    rights_ring.turn(1)
    lefts_ring.turn(1, (0,))
    rights_ring.turn(2)
    lefts_ring.turn(1, (1,))
    rights_ring.turn(3)
    lefts_ring.turn(2)
    rights_ring.turn(4)

    for ch in range(8):
        lefts = jnp.concatenate([left_all[s, ch] for s in range(ZS)], 0)
        rights = jnp.concatenate([right_all[s, ch] for s in range(YS)], 0)
        tri_work[64 * ch : 64 * ch + 64, :] = dot(lefts, rights, 1, 1)
    pieces = [
        jnp.concatenate([tri_work[pl.ds(8 * g + m, 8, stride=64), :] for g in range(8)], 0)
        for m in range(8)
    ]
    pieces = swap_blocks(pieces, 16)
    for s in range(YS):
        for h in range(2):
            four = [pieces[s][8 * (4 * h + g) : 8 * (4 * h + g) + 8] for g in range(4)]
            rows = [jnp.concatenate(four[:2], 1), jnp.concatenate(four[2:], 1)]
            tri_send[h * YS + s] = jnp.concatenate(rows, 0).astype(BF16)

    @pl.loop(0, 2 * YS)
    def _(s):
        h = s // YS
        row, yy = 2 * y + h, (y + s) % YS
        itself = jnp.logical_and(row == r, yy == y)
        at = h * YS + yy

        @pl.when(jnp.logical_not(itself))
        def _():
            send(tri_send.at[at], tri_recv.at[r], tri_ss.at[at], tri_rs.at[r], row, yy * ZS + z)

        @pl.when(itself)
        def _():
            tri_recv[r] = tri_send[at]

    @pl.loop(0, ROWS)
    def _(s):
        @pl.when(jnp.logical_or(s != r, r // 2 != y))
        def _():
            wait(tri_recv.at[s], tri_rs.at[s])

    arrived = tri_recv[...].astype(F32)
    tri_t = jnp.concatenate(
        [arrived[:, :8].reshape(128, 256), arrived[:, 8:].reshape(128, 256)], 1
    )
    gain_col = jnp.broadcast_to(gain_mid[...], (128, 128)).T
    tri_normed = layer_norm(tri_t, jnp.concatenate([gain_col] * 4, 1), 0).astype(BF16)
    update = gate_tri[...] * dot(tri_normed, w_tri_out[...], 0, 0)
    pair_one = (pair_ref[...].astype(F32).reshape(512, 128) + update).astype(BF16)
    work[...] = pair_one.astype(F32)
    pair_t = jnp.concatenate([work[pl.ds(j, 32, stride=16), :] for j in range(16)], 0)
    pair_one_t[...] = pair_t

    normed_two = layer_norm(pair_t, gain_att[...]).astype(BF16)
    bias_t = dot(w_bias[...], normed_two, 1, 1)
    sub = lax.broadcasted_iota(jnp.int32, (16, 128), 0)
    for h in range(HEADS):
        base = jnp.zeros((16, 128), F32)
        for v in range(4):
            base = jnp.where(
                sub == v,
                jnp.broadcast_to(bias_t[h : h + 1, 128 * v : 128 * v + 128], (16, 128)),
                base,
            )
        for g in range(4):
            row = jnp.broadcast_to(mask[:, 128 * g : 128 * g + 128], (16, 128))
            bias_send[4 * h + g] = jnp.where(sub == 4, row, base).astype(BF16)
    bias_recv[r] = bias_send[r]

    @pl.loop(1, ROWS)
    def _(s):
        to = (r + s) % ROWS
        send(bias_send.at[to], bias_recv.at[r], bias_ss.at[to], bias_rs.at[r], to, c)

    projected = dot(w_attend[...], normed_two, 0, 1)
    for h in range(HEADS):
        for part in range(3):
            rows = projected[128 * part + 32 * h : 128 * part + 32 * h + 32]
            if part == 0:
                rows = rows * (LOG2E / math.sqrt(HEAD_DIM))
            for g in range(4):
                qkv_send[4 * h + g, 32 * part : 32 * part + 32, :] = rows[
                    :, 128 * g : 128 * g + 128
                ].astype(BF16)
    qkv_recv[r] = qkv_send[r]

    @pl.loop(1, ROWS)
    def _(s):
        to = (r + s) % ROWS
        send(qkv_send.at[to], qkv_recv.at[r], qkv_ss.at[to], qkv_rs.at[r], to, c)

    gate_att[...] = jax.nn.sigmoid(projected[384:])

    @pl.loop(1, ROWS)
    def _(s):
        of = (r + s) % ROWS
        wait(bias_recv.at[of], bias_rs.at[of])

    pieces = [
        jnp.concatenate([bias_recv[4 * a + b].astype(F32) for a in range(4)], 0) for b in range(4)
    ]
    for q, piece in enumerate(swap_blocks(pieces, 32)):
        for a in range(4):
            for v in range(4):
                bias_work[a, 4 * v + q : 4 * v + q + 1, :] = piece[16 * a + v : 16 * a + v + 1]
            mask_cols[q, 0:1, 128 * a : 128 * a + 128] = piece[16 * a + 4 : 16 * a + 5]
    for a in range(4):
        bias_all[y, z, :, 128 * a : 128 * a + 128] = bias_work[a].astype(BF16)

    @pl.loop(1, ZS)
    def _(s):
        to = (z + s) % ZS
        send(bias_all.at[y, z], bias_all.at[y, z], biasz_ss.at[to], biasz_rs.at[z], r, y * ZS + to)

    @pl.loop(1, ZS)
    def _(s):
        of = (z + s) % ZS
        wait(bias_all.at[y, of], biasz_rs.at[of])

    bias_ring.start()

    @pl.loop(1, ROWS)
    def _(s):
        of = (r + s) % ROWS
        wait(qkv_recv.at[of], qkv_rs.at[of])

    tail = (lax.broadcasted_iota(jnp.int32, (16, 512), 0) == 0).astype(BF16)
    for q in range(4):
        value_buf[q, 32:48, :] = tail
    for a in range(4):
        pieces = [qkv_recv[4 * a + b].astype(F32) for b in range(4)]
        for q, piece in enumerate(swap_blocks(pieces, 32)):
            piece = piece.astype(BF16)
            query_buf[q, a] = piece[:32]
            key_buf[q, :, 128 * a : 128 * a + 128] = piece[32:64]
            value_buf[q, 0:32, 128 * a : 128 * a + 128] = piece[64:]

    side = 1 - 2 * (y % 2)
    for step, apart in enumerate((0, -side, side, 2)):
        bias_ring.turn(step + 1)
        a = (y // 2 + 4 + apart) % 4
        bias_full[...] = bias_all[pl.ds(2 * a, 2)].astype(F32).reshape(128, 512) * LOG2E
        pieces = []
        for q in range(4):
            scores = dot(query_buf[q, a], key_buf[q], 0, 0) + bias_full[...]
            scores = jnp.where(mask_cols[q, 0:1, :] > 0.5, scores, MASKED)
            weight = jnp.exp2(scores - jnp.max(scores, 1, keepdims=True)).astype(BF16)
            total = dot(value_buf[q], weight, 1, 1)
            pieces.append(total[:32] / total[32:33])
        for b, piece in enumerate(swap_blocks(pieces, 32)):
            at = 4 * a + b
            att_send[at] = piece.astype(BF16)

            @pl.when(r != at)
            def _():
                send(att_send.at[at], att_recv.at[r], att_ss.at[at], att_rs.at[r], at, c)

            @pl.when(r == at)
            def _():
                att_recv[r] = att_send[at]

    @pl.loop(1, ROWS)
    def _(s):
        of = (r + s) % ROWS
        wait(att_recv.at[of], att_rs.at[of])

    attended = jnp.concatenate(
        [
            jnp.concatenate([att_recv[4 * h + g].astype(F32) for g in range(4)], 1)
            for h in range(HEADS)
        ],
        0,
    )
    gated = (gate_att[...] * attended).astype(BF16)
    pair_two = (pair_one_t[...] + dot(gated, w_attend_out[...], 0, 0)).astype(BF16).astype(F32)
    normed_three = layer_norm(pair_two, gain_trans[...]).astype(BF16)
    for part in range(4):
        rows = slice(128 * part, 128 * part + 128)
        expanded = dot(normed_three[rows], w_trans_in[...], 1, 0)
        hidden = (jax.nn.silu(expanded[:, :512]) * expanded[:, 512:]).astype(BF16)
        work[rows, :] = pair_two[rows] + dot(hidden, w_trans_out[...], 1, 0)
    for i in range(32):
        out_ref[i] = work[pl.ds(i, 16, stride=32), :].astype(BF16)

    @pl.loop(1, ROWS)
    def _(s):
        to = (r + s) % ROWS
        wait(edge_send.at[to], edge_ss.at[to])
        wait(bias_send.at[to], bias_ss.at[to])
        wait(qkv_send.at[to], qkv_ss.at[to])
        wait(att_send.at[to], att_ss.at[to])

    @pl.loop(1, ZS)
    def _(s):
        to = (z + s) % ZS
        wait(bias_all.at[0, 0], biasz_ss.at[to])

    @pl.loop(0, 2 * YS)
    def _(s):
        @pl.when(jnp.logical_or(2 * y + s // YS != r, s % YS != y))
        def _():
            wait(tri_send.at[s], tri_ss.at[s])

    for each in (rights_ring, lefts_ring, bias_ring):
        each.sent()


def per_device(
    pair, pair_mask, gain_tri, w_left, w_right, w_tri_gate, gain_mid, w_tri_out, gain_att, w_attend,
    w_bias, w_attend_out, gain_trans, w_trans_in, w_trans_out,
):
    vmem = pl.BlockSpec(memory_space=pltpu.VMEM)
    dma = pltpu.SemaphoreType.DMA
    row = lambda gain: gain.reshape(1, 128)
    return pl.pallas_call(
        kernel,
        out_shape=jax.ShapeDtypeStruct((32, 16, 128), BF16),
        in_specs=[pl.BlockSpec(memory_space=pltpu.HBM)] * 15,
        out_specs=vmem,
        scratch_shapes=[
            pltpu.VMEM((32, 16, 128), BF16),
            pltpu.VMEM((16, 32), jnp.int32),
            pltpu.VMEM((1, 128), F32),
            pltpu.VMEM((128, 256), BF16),
            pltpu.VMEM((128, 256), BF16),
            pltpu.VMEM((128, 128), BF16),
            pltpu.VMEM((1, 128), F32),
            pltpu.VMEM((128, 128), BF16),
            pltpu.VMEM((1, 128), F32),
            pltpu.VMEM((128, 512), BF16),
            pltpu.VMEM((4, 128), BF16),
            pltpu.VMEM((128, 128), BF16),
            pltpu.VMEM((1, 128), F32),
            pltpu.VMEM((128, 1024), BF16),
            pltpu.VMEM((512, 128), BF16),
            dma((15,)),
            pltpu.VMEM((512, 128), F32),
            pltpu.VMEM((16, 16, 512), BF16),
            pltpu.VMEM((16, 16, 512), BF16),
            pltpu.VMEM((4, 256, 128), F32),
            pltpu.VMEM((ZS, 8, 16, 512), BF16),
            pltpu.VMEM((YS, 8, 16, 512), BF16),
            pltpu.VMEM((512, 128), F32),
            pltpu.VMEM((512, 128), F32),
            pltpu.VMEM((16, 16, 256), BF16),
            pltpu.VMEM((16, 16, 256), BF16),
            pltpu.VMEM((16, 16, 128), BF16),
            pltpu.VMEM((16, 16, 128), BF16),
            pltpu.VMEM((4, 16, 128), F32),
            pltpu.VMEM((YS, ZS, 16, 512), BF16),
            pltpu.VMEM((128, 512), F32),
            pltpu.VMEM((4, 8, 512), F32),
            pltpu.VMEM((512, 128), F32),
            pltpu.VMEM((128, 512), F32),
            pltpu.VMEM((16, 96, 128), BF16),
            pltpu.VMEM((16, 96, 128), BF16),
            pltpu.VMEM((4, 4, 32, 128), BF16),
            pltpu.VMEM((4, 32, 512), BF16),
            pltpu.VMEM((4, 48, 512), BF16),
            pltpu.VMEM((16, 32, 128), BF16),
            pltpu.VMEM((16, 32, 128), BF16),
            dma((16,)), dma((16,)),
            dma((2, 5, 2)), dma((2, 5, 2)),
            dma((2, 5, 2)), dma((2, 5, 2)),
            dma((16,)), dma((16,)),
            dma((16,)), dma((16,)),
            dma((ZS,)), dma((ZS,)),
            dma((2, 5, 2)), dma((2, 5, 2)),
            dma((16,)), dma((16,)),
            dma((16,)), dma((16,)),
        ],
        compiler_params=pltpu.CompilerParams(
            collective_id=0, has_side_effects=True, vmem_limit_bytes=VMEM_LIMIT
        ),
    )(
        pair, pair_mask.T, row(gain_tri), w_left, w_right, w_tri_gate, row(gain_mid),
        w_tri_out, row(gain_att), w_attend, w_bias.T, w_attend_out, row(gain_trans), w_trans_in,
        w_trans_out,
    )


def solution(mesh):
    in_specs = (P("row", "col", None), P("row", "col")) + (P(),) * 13
    return jax.shard_map(
        per_device, mesh=mesh, in_specs=in_specs, out_specs=P("row", "col", None), check_vma=False
    )
```

time: 254 us -> 82.2 us (0.32)
  the two profiles are of different devices: /device:TPU:1 before, /device:TPU:67 now
where the time goes in v2:
time: 82.2 us; the launch traced here: 82.1 us
  Pallas kernels  80.5 us (98%)
  local copies, waits for them, and re-layouts  1.57 us (2%)
    pallas_call x1, Pallas kernels, per_device(): pl.pallas_call(kernel, out_shape=jax.ShapeDtypeStruct((32, 16, 128), BF16...  80.5 us

profile of v2, /device:TPU:67, one launch (start us, length us, event | category | flops | bytes accessed | tf_op | source)
XLA Modules:
  0.0 82.1 jit_solution(6819689657112159930)
XLA Ops:
  0.0 80.5 %shard_map.145 = bf16[32,16,128]{2,1,0:T(8,128)(2,1)} custom-call(bf16[32,16,128]{2,1,0:T(8,128)(2,1)} %pair_hbm.1, s32[16,32]{1,0:T(8,128)} %bitcast.6, f32[1,128]{1,0:T(1,128)} %bitcast.8, bf16[128,256]{1,0:T(8,128)(2,1)} %w_left_hbm.1, bf16[128,256]{1,0:T(8,128)(2,1)} %w_right_hbm.1, bf16[128,128]{1,0:T(8,128)(2,1)} %w_tri_gate_hbm.1, f32[1,128]{1,0:T(1,128)} %bitcast.9, ...), custom_call_target="tpu_custom_call" | custom-call | tf_op jit(solution)/shard_map/pallas_call | solution.py:449
  80.5 1.6 %copy.17 = bf16[32,16,128]{2,1,0:T(8,128)(2,1)} copy(bf16[32,16,128]{2,1,0:T(8,128)(2,1)} %shard_map.145) | data formatting | bytes 262144

commit v3 on v2

--- a/solution.py
+++ b/solution.py
@@ -235,37 +235,51 @@
     lefts_ring.turn(1, (1,))
     rights_ring.turn(3)
     lefts_ring.turn(2)
+    def reply(slot, piece):
+        yy = (y + YS + slot - 3) % YS
+        for h in range(2):
+            four = [piece[8 * (4 * h + g) : 8 * (4 * h + g) + 8] for g in range(4)]
+            rows = [jnp.concatenate(four[:2], 1), jnp.concatenate(four[2:], 1)]
+            at = h * YS + yy
+            tri_send[at] = jnp.concatenate(rows, 0).astype(BF16)
+            row = 2 * y + h
+            if slot == 3:
+
+                @pl.when(row != r)
+                def _():
+                    send(tri_send.at[at], tri_recv.at[r], tri_ss.at[at], tri_rs.at[r], row, c)
+
+                @pl.when(row == r)
+                def _():
+                    tri_recv[r] = tri_send[at]
+
+            else:
+                send(
+                    tri_send.at[at], tri_recv.at[r], tri_ss.at[at], tri_rs.at[r], row, yy * ZS + z
+                )
+
+    def products(slots):
+        for ch in range(8):
+            lefts = jnp.concatenate([left_all[s, ch] for s in range(ZS)], 0)
+            rights = [right_all[(y + YS + s - 3) % YS, ch] for s in slots]
+            found = dot(lefts, jnp.concatenate(rights, 0), 1, 1)
+            tri_work[64 * ch : 64 * ch + 64, 0 : 16 * len(rights)] = found
+        return [
+            jnp.concatenate([tri_work[pl.ds(8 * g + m, 8, stride=64), :] for g in range(8)], 0)
+            for m in range(8)
+        ]
+
+    tri_work[...] = jnp.zeros_like(tri_work)
+    pieces = swap_blocks(products(range(7)), 16)
+    for slot in (2, 4, 1, 5, 0, 6, 3):
+        reply(slot, pieces[slot])
     rights_ring.turn(4)
-
-    for ch in range(8):
-        lefts = jnp.concatenate([left_all[s, ch] for s in range(ZS)], 0)
-        rights = jnp.concatenate([right_all[s, ch] for s in range(YS)], 0)
-        tri_work[64 * ch : 64 * ch + 64, :] = dot(lefts, rights, 1, 1)
-    pieces = [
-        jnp.concatenate([tri_work[pl.ds(8 * g + m, 8, stride=64), :] for g in range(8)], 0)
-        for m in range(8)
-    ]
-    pieces = swap_blocks(pieces, 16)
-    for s in range(YS):
-        for h in range(2):
-            four = [pieces[s][8 * (4 * h + g) : 8 * (4 * h + g) + 8] for g in range(4)]
-            rows = [jnp.concatenate(four[:2], 1), jnp.concatenate(four[2:], 1)]
-            tri_send[h * YS + s] = jnp.concatenate(rows, 0).astype(BF16)
-
-    @pl.loop(0, 2 * YS)
-    def _(s):
-        h = s // YS
-        row, yy = 2 * y + h, (y + s) % YS
-        itself = jnp.logical_and(row == r, yy == y)
-        at = h * YS + yy
-
-        @pl.when(jnp.logical_not(itself))
-        def _():
-            send(tri_send.at[at], tri_recv.at[r], tri_ss.at[at], tri_rs.at[r], row, yy * ZS + z)
-
-        @pl.when(itself)
-        def _():
-            tri_recv[r] = tri_send[at]
+    pieces = products([7])
+    lane = lax.broadcasted_iota(jnp.int32, pieces[0].shape, 1) >> 4
+    merged = pieces[0]
+    for m in range(1, 8):
+        merged = jnp.where(lane == m, pltpu.roll(pieces[m], 16 * m, 1), merged)
+    reply(7, merged)
 
     @pl.loop(0, ROWS)
     def _(s):
@@ -352,12 +366,14 @@
         wait(bias_all.at[y, of], biasz_rs.at[of])
 
     bias_ring.start()
+    bias_ring.turn(1)
 
     @pl.loop(1, ROWS)
     def _(s):
         of = (r + s) % ROWS
         wait(qkv_recv.at[of], qkv_rs.at[of])
 
+    bias_ring.turn(2)
     tail = (lax.broadcasted_iota(jnp.int32, (16, 512), 0) == 0).astype(BF16)
     for q in range(4):
         value_buf[q, 32:48, :] = tail
@@ -371,7 +387,8 @@
 
     side = 1 - 2 * (y % 2)
     for step, apart in enumerate((0, -side, side, 2)):
-        bias_ring.turn(step + 1)
+        if step in (1, 3):
+            bias_ring.turn(3 + step // 2)
         a = (y // 2 + 4 + apart) % 4
         bias_full[...] = bias_all[pl.ds(2 * a, 2)].astype(F32).reshape(128, 512) * LOG2E
         pieces = []
@@ -448,7 +465,7 @@
     row = lambda gain: gain.reshape(1, 128)
     return pl.pallas_call(
         kernel,
-        out_shape=jax.ShapeDtypeStruct((32, 16, 128), BF16),
+        out_shape=pltpu.VMEM((32, 16, 128), BF16),
         in_specs=[pl.BlockSpec(memory_space=pltpu.HBM)] * 15,
         out_specs=vmem,
         scratch_shapes=[

time: 82.2 us -> 80.3 us (0.977)
  the two profiles are of different devices: /device:TPU:67 before, /device:TPU:65 now
where the time goes in v3:
time: 80.3 us; the launch traced here: 80.2 us
  Pallas kernels  79.5 us (99%)
    pallas_call x1, Pallas kernels, per_device(): pl.pallas_call(kernel, out_shape=pltpu.VMEM((32, 16, 128), BF16), in_spec...  79.5 us

profile of v3, /device:TPU:65, one launch (start us, length us, event | category | flops | bytes accessed | tf_op | source)
XLA Modules:
  0.0 80.2 jit_solution(3233969630554714232)
XLA Ops:
  0.0 79.5 %shard_map.145 = bf16[32,16,128]{2,1,0:T(8,128)(2,1)S(1)} custom-call(bf16[32,16,128]{2,1,0:T(8,128)(2,1)} %pair_hbm.1, s32[16,32]{1,0:T(8,128)} %bitcast.6, f32[1,128]{1,0:T(1,128)} %bitcast.8, bf16[128,256]{1,0:T(8,128)(2,1)} %w_left_hbm.1, bf16[128,256]{1,0:T(8,128)(2,1)} %w_right_hbm.1, bf16[128,128]{1,0:T(8,128)(2,1)} %w_tri_gate_hbm.1, ...), custom_call_target="tpu_custom_call" | custom-call | tf_op jit(solution)/shard_map/pallas_call | solution.py:466
  79.5 0.7 copy.17

commit v4 on v3

--- a/solution.py
+++ b/solution.py
@@ -59,18 +59,18 @@
     out_ref,
     pair_ref, mask_ref, gain_tri, w_left, w_right, w_tri_gate, gain_mid, w_tri_out, gain_att,
     w_attend, w_bias, w_attend_out, gain_trans, w_trans_in, w_trans_out, load_sems,
-    work, edge_send, edge_recv, edge_work, left_all, right_all, gate_tri, tri_work, tri_send,
+    work, edge_send, edge_recv, edge_work, near_all, far_all, gate_tri, tri_work, tri_send,
     tri_recv, bias_send, bias_recv, bias_work, bias_all, bias_full, mask_cols, pair_one_t, gate_att,
     qkv_send, qkv_recv, query_buf, key_buf, value_buf, att_send, att_recv,
-    edge_ss, edge_rs, left_ss, left_rs, right_ss, right_rs, tri_ss, tri_rs, bias_ss, bias_rs,
+    edge_ss, edge_rs, near_ss, near_rs, far_ss, far_rs, tri_ss, tri_rs, bias_ss, bias_rs,
     biasz_ss, biasz_rs, biasy_ss, biasy_rs, qkv_ss, qkv_rs, att_ss, att_rs,
 ):
     r = lax.axis_index("row")
     c = lax.axis_index("col")
-    y = c // ZS
-    z = c % ZS
-    up = ((y + 1) % YS) * ZS + z
-    down = ((y + YS - 1) % YS) * ZS + z
+    y = c >> 2
+    z = c & (ZS - 1)
+    up = ((y + 1) & (YS - 1)) * ZS + z
+    down = ((y + YS - 1) & (YS - 1)) * ZS + z
 
     def send(src, dst, ssem, rsem, row, col):
         pltpu.make_async_remote_copy(
@@ -104,35 +104,21 @@
 
     @pl.loop(1, ROWS)
     def _(s):
-        hello((r + s) % ROWS, c)
+        hello((r + s) & (ROWS - 1), c)
 
     @pl.loop(1, ZS)
     def _(s):
-        hello(r, y * ZS + (z + s) % ZS)
+        hello(r, y * ZS + ((z + s) & (ZS - 1)))
 
     hello(r, up)
     hello(r, down)
 
-    @pl.loop(0, 2 * YS)
-    def _(s):
-        row, yy = 2 * y + s // YS, s % YS
-
-        @pl.when(jnp.logical_or(row != r, yy != y))
-        def _():
-            hello(row, yy * ZS + z)
-
-    @pl.loop(0, ROWS)
-    def _(s):
-        @pl.when(jnp.logical_or(s != r, r // 2 != y))
-        def _():
-            hello(s, (r // 2) * ZS + z)
-
     for load in loads[:5]:
         load.wait()
-    pair = pair_ref[...].astype(F32).reshape(512, 128)
-    normed = layer_norm(pair, gain_tri[...]).astype(BF16)
-    work[...] = normed.astype(F32)
-    normed_t = jnp.concatenate([work[pl.ds(j, 32, stride=16), :] for j in range(16)], 0).astype(BF16)
+    work[...] = pair_ref[...].astype(F32).reshape(512, 128)
+    pair_t = jnp.concatenate([work[pl.ds(j, 32, stride=16), :] for j in range(16)], 0)
+    pair_one_t[...] = pair_t
+    normed_t = layer_norm(pair_t, gain_tri[...]).astype(BF16)
     lane = lax.broadcasted_iota(jnp.int32, (32, 512), 1)
     spread = lax.broadcasted_iota(jnp.int32, (32, 512), 0) == (lane & 31)
     mask = dot(mask_ref[...].astype(F32).astype(BF16), spread.astype(F32).astype(BF16), 1, 0)
@@ -140,29 +126,26 @@
     own = lax.broadcasted_iota(jnp.int32, (16, 512), 0) == (lane >> 5)
     mask = jnp.sum(jnp.where(own, mask, 0.0), 0, keepdims=True)
     sides = []
-    for weight in (w_left, w_right):
+    for weight in (w_right, w_left):
         projected = dot(weight[...], normed_t, 0, 1)
         sides.append((mask * jax.nn.sigmoid(projected[:128]) * projected[128:]).reshape(ROWS, 8, 512))
     edge_send[...] = jnp.concatenate(sides, 1).astype(BF16)
     edge_recv[r] = edge_send[r]
 
-    pl.semaphore_wait(
-        barrier,
-        (ROWS - 1) + (ZS - 1) + 2 + 2 * (2 * YS) - jnp.where(r // 2 == y, 2, 0),
-    )
-
-    @pl.loop(1, ROWS)
-    def _(s):
-        to = (r + s) % ROWS
+    pl.semaphore_wait(barrier, (ROWS - 1) + (ZS - 1) + 2)
+
+    @pl.loop(1, ROWS)
+    def _(s):
+        to = (r + s) & (ROWS - 1)
         send(edge_send.at[to], edge_recv.at[r], edge_ss.at[to], edge_rs.at[r], to, c)
 
     for load in loads[5:]:
         load.wait()
-    gate_tri[...] = jax.nn.sigmoid(dot(normed, w_tri_gate[...], 1, 0))
-
-    @pl.loop(1, ROWS)
-    def _(s):
-        of = (r + s) % ROWS
+    gate_tri[...] = jax.nn.sigmoid(dot(normed_t, w_tri_gate[...], 1, 0))
+
+    @pl.loop(1, ROWS)
+    def _(s):
+        of = (r + s) & (ROWS - 1)
         wait(edge_recv.at[of], edge_rs.at[of])
 
     for v in range(4):
@@ -177,8 +160,8 @@
                 edge_work.at[a][pl.ds(4 * v + q, 16, stride=16), :] = piece[16 * a : 16 * a + 16]
     for a in range(4):
         block = edge_work[a].astype(BF16).reshape(2, 8, 16, 128)
-        left_all[z, :, :, 128 * a : 128 * a + 128] = block[0]
-        right_all[y, :, :, 128 * a : 128 * a + 128] = block[1]
+        near_all[z, :, :, 128 * a : 128 * a + 128] = block[0]
+        far_all[y, :, :, 128 * a : 128 * a + 128] = block[1]
 
     class Ring:
         def __init__(self, buf, ss, rs, size, me, to):
@@ -186,7 +169,7 @@
             self.half = buf.shape[1] // 2
 
         def part(self, block, chunk):
-            return self.buf.at[block % self.size, pl.ds(chunk * self.half, self.half)]
+            return self.buf.at[block & (self.size - 1), pl.ds(chunk * self.half, self.half)]
 
         def send(self, step, chunk, way):
             block = self.me + self.size - step + 1 if way == 0 else self.me + step - 1
@@ -221,49 +204,49 @@
                             wait(self.part(0, 0), self.ss.at[way, step, chunk])
 
     y_ring = ((r, up), (r, down))
-    rights_ring = Ring(right_all, right_ss, right_rs, YS, y, y_ring)
-    lefts_ring = Ring(
-        left_all, left_ss, left_rs, ZS, z,
-        ((r, y * ZS + (z + 1) % ZS), (r, y * ZS + (z + ZS - 1) % ZS)),
+    far_ring = Ring(far_all, far_ss, far_rs, YS, y, y_ring)
+    near_ring = Ring(
+        near_all, near_ss, near_rs, ZS, z,
+        ((r, y * ZS + ((z + 1) & (ZS - 1))), (r, y * ZS + ((z + ZS - 1) & (ZS - 1)))),
     )
     bias_ring = Ring(bias_all, biasy_ss, biasy_rs, YS, y, y_ring)
-    rights_ring.start()
-    lefts_ring.start()
-    rights_ring.turn(1)
-    lefts_ring.turn(1, (0,))
-    rights_ring.turn(2)
-    lefts_ring.turn(1, (1,))
-    rights_ring.turn(3)
-    lefts_ring.turn(2)
+    far_ring.start()
+    near_ring.start()
+    far_ring.turn(1)
+    near_ring.turn(1, (0,))
+    far_ring.turn(2)
+    near_ring.turn(1, (1,))
+    far_ring.turn(3)
+    near_ring.turn(2)
     def reply(slot, piece):
-        yy = (y + YS + slot - 3) % YS
-        for h in range(2):
-            four = [piece[8 * (4 * h + g) : 8 * (4 * h + g) + 8] for g in range(4)]
-            rows = [jnp.concatenate(four[:2], 1), jnp.concatenate(four[2:], 1)]
-            at = h * YS + yy
-            tri_send[at] = jnp.concatenate(rows, 0).astype(BF16)
-            row = 2 * y + h
-            if slot == 3:
-
-                @pl.when(row != r)
-                def _():
-                    send(tri_send.at[at], tri_recv.at[r], tri_ss.at[at], tri_rs.at[r], row, c)
-
-                @pl.when(row == r)
-                def _():
-                    tri_recv[r] = tri_send[at]
-
-            else:
-                send(
-                    tri_send.at[at], tri_recv.at[r], tri_ss.at[at], tri_rs.at[r], row, yy * ZS + z
-                )
+        yy = (y + YS + slot - 3) & (YS - 1)
+        tri_send[yy] = piece.astype(BF16).reshape(ZS, 16, 128)
+        row = 2 * yy + (z >> 1)
+        half = z & 1
+        for t in (1, 2, 3):
+            zz = (z + t) & (ZS - 1)
+            send(
+                tri_send.at[yy, zz], tri_recv.at[half, r], tri_ss.at[yy, zz], tri_rs.at[half, r],
+                row, y * ZS + zz,
+            )
+
+        @pl.when(row != r)
+        def _():
+            send(
+                tri_send.at[yy, z], tri_recv.at[half, r], tri_ss.at[yy, z], tri_rs.at[half, r],
+                row, c,
+            )
+
+        @pl.when(row == r)
+        def _():
+            tri_recv[half, r] = tri_send[yy, z]
 
     def products(slots):
         for ch in range(8):
-            lefts = jnp.concatenate([left_all[s, ch] for s in range(ZS)], 0)
-            rights = [right_all[(y + YS + s - 3) % YS, ch] for s in slots]
-            found = dot(lefts, jnp.concatenate(rights, 0), 1, 1)
-            tri_work[64 * ch : 64 * ch + 64, 0 : 16 * len(rights)] = found
+            rights = jnp.concatenate([near_all[s, ch] for s in range(ZS)], 0)
+            lefts = [far_all[(y + YS + s - 3) & (YS - 1), ch] for s in slots]
+            found = dot(rights, jnp.concatenate(lefts, 0), 1, 1)
+            tri_work[64 * ch : 64 * ch + 64, 0 : 16 * len(lefts)] = found
         return [
             jnp.concatenate([tri_work[pl.ds(8 * g + m, 8, stride=64), :] for g in range(8)], 0)
             for m in range(8)
@@ -273,7 +256,7 @@
     pieces = swap_blocks(products(range(7)), 16)
     for slot in (2, 4, 1, 5, 0, 6, 3):
         reply(slot, pieces[slot])
-    rights_ring.turn(4)
+    far_ring.turn(4)
     pieces = products([7])
     lane = lax.broadcasted_iota(jnp.int32, pieces[0].shape, 1) >> 4
     merged = pieces[0]
@@ -283,20 +266,32 @@
 
     @pl.loop(0, ROWS)
     def _(s):
-        @pl.when(jnp.logical_or(s != r, r // 2 != y))
-        def _():
-            wait(tri_recv.at[s], tri_rs.at[s])
-
-    arrived = tri_recv[...].astype(F32)
+        for half in range(2):
+
+            @pl.when(jnp.logical_or(s != r, z != 2 * (r & 1) + half))
+            def _():
+                wait(tri_recv.at[half, s], tri_rs.at[half, s])
+
     tri_t = jnp.concatenate(
-        [arrived[:, :8].reshape(128, 256), arrived[:, 8:].reshape(128, 256)], 1
+        [
+            tri_recv[half].astype(F32)[:, 8 * g : 8 * g + 8].reshape(128, 128)
+            for half in range(2)
+            for g in range(2)
+        ],
+        1,
     )
     gain_col = jnp.broadcast_to(gain_mid[...], (128, 128)).T
     tri_normed = layer_norm(tri_t, jnp.concatenate([gain_col] * 4, 1), 0).astype(BF16)
-    update = gate_tri[...] * dot(tri_normed, w_tri_out[...], 0, 0)
-    pair_one = (pair_ref[...].astype(F32).reshape(512, 128) + update).astype(BF16)
-    work[...] = pair_one.astype(F32)
-    pair_t = jnp.concatenate([work[pl.ds(j, 32, stride=16), :] for j in range(16)], 0)
+    update = dot(tri_normed, w_tri_out[...], 0, 0)
+    update = jnp.concatenate(
+        [
+            update[256 * half + 16 * j : 256 * half + 16 * j + 16]
+            for j in range(16)
+            for half in range(2)
+        ],
+        0,
+    )
+    pair_t = (pair_one_t[...] + gate_tri[...] * update).astype(BF16).astype(F32)
     pair_one_t[...] = pair_t
 
     normed_two = layer_norm(pair_t, gain_att[...]).astype(BF16)
@@ -317,7 +312,7 @@
 
     @pl.loop(1, ROWS)
     def _(s):
-        to = (r + s) % ROWS
+        to = (r + s) & (ROWS - 1)
         send(bias_send.at[to], bias_recv.at[r], bias_ss.at[to], bias_rs.at[r], to, c)
 
     projected = dot(w_attend[...], normed_two, 0, 1)
@@ -334,14 +329,14 @@
 
     @pl.loop(1, ROWS)
     def _(s):
-        to = (r + s) % ROWS
+        to = (r + s) & (ROWS - 1)
         send(qkv_send.at[to], qkv_recv.at[r], qkv_ss.at[to], qkv_rs.at[r], to, c)
 
     gate_att[...] = jax.nn.sigmoid(projected[384:])
 
     @pl.loop(1, ROWS)
     def _(s):
-        of = (r + s) % ROWS
+        of = (r + s) & (ROWS - 1)
         wait(bias_recv.at[of], bias_rs.at[of])
 
     pieces = [
@@ -357,12 +352,12 @@
 
     @pl.loop(1, ZS)
     def _(s):
-        to = (z + s) % ZS
+        to = (z + s) & (ZS - 1)
         send(bias_all.at[y, z], bias_all.at[y, z], biasz_ss.at[to], biasz_rs.at[z], r, y * ZS + to)
 
     @pl.loop(1, ZS)
     def _(s):
-        of = (z + s) % ZS
+        of = (z + s) & (ZS - 1)
         wait(bias_all.at[y, of], biasz_rs.at[of])
 
     bias_ring.start()
@@ -370,7 +365,7 @@
 
     @pl.loop(1, ROWS)
     def _(s):
-        of = (r + s) % ROWS
+        of = (r + s) & (ROWS - 1)
         wait(qkv_recv.at[of], qkv_rs.at[of])
 
     bias_ring.turn(2)
@@ -385,11 +380,11 @@
             key_buf[q, :, 128 * a : 128 * a + 128] = piece[32:64]
             value_buf[q, 0:32, 128 * a : 128 * a + 128] = piece[64:]
 
-    side = 1 - 2 * (y % 2)
+    side = 1 - 2 * (y & 1)
     for step, apart in enumerate((0, -side, side, 2)):
         if step in (1, 3):
             bias_ring.turn(3 + step // 2)
-        a = (y // 2 + 4 + apart) % 4
+        a = ((y >> 1) + 4 + apart) & 3
         bias_full[...] = bias_all[pl.ds(2 * a, 2)].astype(F32).reshape(128, 512) * LOG2E
         pieces = []
         for q in range(4):
@@ -412,7 +407,7 @@
 
     @pl.loop(1, ROWS)
     def _(s):
-        of = (r + s) % ROWS
+        of = (r + s) & (ROWS - 1)
         wait(att_recv.at[of], att_rs.at[of])
 
     attended = jnp.concatenate(
@@ -435,7 +430,7 @@
 
     @pl.loop(1, ROWS)
     def _(s):
-        to = (r + s) % ROWS
+        to = (r + s) & (ROWS - 1)
         wait(edge_send.at[to], edge_ss.at[to])
         wait(bias_send.at[to], bias_ss.at[to])
         wait(qkv_send.at[to], qkv_ss.at[to])
@@ -443,16 +438,18 @@
 
     @pl.loop(1, ZS)
     def _(s):
-        to = (z + s) % ZS
+        to = (z + s) & (ZS - 1)
         wait(bias_all.at[0, 0], biasz_ss.at[to])
 
-    @pl.loop(0, 2 * YS)
-    def _(s):
-        @pl.when(jnp.logical_or(2 * y + s // YS != r, s % YS != y))
-        def _():
-            wait(tri_send.at[s], tri_ss.at[s])
-
-    for each in (rights_ring, lefts_ring, bias_ring):
+    @pl.loop(0, YS)
+    def _(s):
+        for t in range(ZS):
+
+            @pl.when(jnp.logical_or(2 * s + (z >> 1) != r, z != t))
+            def _():
+                wait(tri_send.at[s, t], tri_ss.at[s, t])
+
+    for each in (far_ring, near_ring, bias_ring):
         each.sent()
 
 
@@ -493,8 +490,8 @@
             pltpu.VMEM((YS, 8, 16, 512), BF16),
             pltpu.VMEM((512, 128), F32),
             pltpu.VMEM((512, 128), F32),
-            pltpu.VMEM((16, 16, 256), BF16),
-            pltpu.VMEM((16, 16, 256), BF16),
+            pltpu.VMEM((YS, ZS, 16, 128), BF16),
+            pltpu.VMEM((2, 16, 16, 128), BF16),
             pltpu.VMEM((16, 16, 128), BF16),
             pltpu.VMEM((16, 16, 128), BF16),
             pltpu.VMEM((4, 16, 128), F32),
@@ -513,7 +510,7 @@
             dma((16,)), dma((16,)),
             dma((2, 5, 2)), dma((2, 5, 2)),
             dma((2, 5, 2)), dma((2, 5, 2)),
-            dma((16,)), dma((16,)),
+            dma((YS, ZS)), dma((2, 16)),
             dma((16,)), dma((16,)),
             dma((ZS,)), dma((ZS,)),
             dma((2, 5, 2)), dma((2, 5, 2)),

time: 80.3 us -> 76.5 us (0.953)
  Pallas kernels: 79.5 us -> 75.7 us
    pallas_call x1, Pallas kernels: 79.5 us -> 75.7 us  [per_device(): pl.pallas_call(kernel, out_shape=pltpu.VMEM((32, 16, 128), BF16), in_spec...]
where the time goes in v4:
time: 76.5 us; the launch traced here: 76.4 us
  Pallas kernels  75.7 us (99%)
    pallas_call x1, Pallas kernels, per_device(): pl.pallas_call(kernel, out_shape=pltpu.VMEM((32, 16, 128), BF16), in_spec...  75.7 us

profile of v4, /device:TPU:65, one launch (start us, length us, event | category | flops | bytes accessed | tf_op | source)
XLA Modules:
  0.0 76.4 jit_solution(9149145301986670373)
XLA Ops:
  0.0 75.7 %shard_map.145 = bf16[32,16,128]{2,1,0:T(8,128)(2,1)S(1)} custom-call(bf16[32,16,128]{2,1,0:T(8,128)(2,1)} %pair_hbm.1, s32[16,32]{1,0:T(8,128)} %bitcast.6, f32[1,128]{1,0:T(1,128)} %bitcast.8, bf16[128,256]{1,0:T(8,128)(2,1)} %w_left_hbm.1, bf16[128,256]{1,0:T(8,128)(2,1)} %w_right_hbm.1, bf16[128,128]{1,0:T(8,128)(2,1)} %w_tri_gate_hbm.1, ...), custom_call_target="tpu_custom_call" | custom-call | tf_op jit(solution)/shard_map/pallas_call | solution.py:463
  75.7 0.7 copy.17

commit v5 on v4

--- a/solution.py
+++ b/solution.py
@@ -61,7 +61,7 @@
     w_attend, w_bias, w_attend_out, gain_trans, w_trans_in, w_trans_out, load_sems,
     work, edge_send, edge_recv, edge_work, near_all, far_all, gate_tri, tri_work, tri_send,
     tri_recv, bias_send, bias_recv, bias_work, bias_all, bias_full, mask_cols, pair_one_t, gate_att,
-    qkv_send, qkv_recv, query_buf, key_buf, value_buf, att_send, att_recv,
+    qkv_send, qkv_recv, query_buf, key_buf, value_buf, normed_buf, att_work, att_send, att_recv,
     edge_ss, edge_rs, near_ss, near_rs, far_ss, far_rs, tri_ss, tri_rs, bias_ss, bias_rs,
     biasz_ss, biasz_rs, biasy_ss, biasy_rs, qkv_ss, qkv_rs, att_ss, att_rs,
 ):
@@ -386,14 +386,16 @@
             bias_ring.turn(3 + step // 2)
         a = ((y >> 1) + 4 + apart) & 3
         bias_full[...] = bias_all[pl.ds(2 * a, 2)].astype(F32).reshape(128, 512) * LOG2E
-        pieces = []
-        for q in range(4):
+
+        @pl.loop(0, 4)
+        def _(q):
             scores = dot(query_buf[q, a], key_buf[q], 0, 0) + bias_full[...]
             scores = jnp.where(mask_cols[q, 0:1, :] > 0.5, scores, MASKED)
             weight = jnp.exp2(scores - jnp.max(scores, 1, keepdims=True)).astype(BF16)
             total = dot(value_buf[q], weight, 1, 1)
-            pieces.append(total[:32] / total[32:33])
-        for b, piece in enumerate(swap_blocks(pieces, 32)):
+            att_work[q] = total[:32] / total[32:33]
+
+        for b, piece in enumerate(swap_blocks([att_work[q] for q in range(4)], 32)):
             at = 4 * a + b
             att_send[at] = piece.astype(BF16)
 
@@ -420,11 +422,16 @@
     gated = (gate_att[...] * attended).astype(BF16)
     pair_two = (pair_one_t[...] + dot(gated, w_attend_out[...], 0, 0)).astype(BF16).astype(F32)
     normed_three = layer_norm(pair_two, gain_trans[...]).astype(BF16)
-    for part in range(4):
-        rows = slice(128 * part, 128 * part + 128)
-        expanded = dot(normed_three[rows], w_trans_in[...], 1, 0)
+    work[...] = pair_two
+    normed_buf[...] = normed_three
+
+    @pl.loop(0, 4)
+    def _(part):
+        rows = pl.ds(pl.multiple_of(128 * part, 128), 128)
+        expanded = dot(normed_buf[rows, :], w_trans_in[...], 1, 0)
         hidden = (jax.nn.silu(expanded[:, :512]) * expanded[:, 512:]).astype(BF16)
-        work[rows, :] = pair_two[rows] + dot(hidden, w_trans_out[...], 1, 0)
+        work[rows, :] = work[rows, :] + dot(hidden, w_trans_out[...], 1, 0)
+
     for i in range(32):
         out_ref[i] = work[pl.ds(i, 16, stride=32), :].astype(BF16)
 
@@ -505,6 +512,8 @@
             pltpu.VMEM((4, 4, 32, 128), BF16),
             pltpu.VMEM((4, 32, 512), BF16),
             pltpu.VMEM((4, 48, 512), BF16),
+            pltpu.VMEM((512, 128), BF16),
+            pltpu.VMEM((4, 32, 128), F32),
             pltpu.VMEM((16, 32, 128), BF16),
             pltpu.VMEM((16, 32, 128), BF16),
             dma((16,)), dma((16,)),

time: 76.5 us -> 78 us (1.020)
  Pallas kernels: 75.7 us -> 77.2 us
    pallas_call x1, Pallas kernels: 75.7 us -> 77.2 us  [per_device(): pl.pallas_call(kernel, out_shape=pltpu.VMEM((32, 16, 128), BF16), in_spec...]
where the time goes in v5:
time: 78 us; the launch traced here: 77.9 us
  Pallas kernels  77.2 us (99%)
    pallas_call x1, Pallas kernels, per_device(): pl.pallas_call(kernel, out_shape=pltpu.VMEM((32, 16, 128), BF16), in_spec...  77.2 us

profile of v5, /device:TPU:65, one launch (start us, length us, event | category | flops | bytes accessed | tf_op | source)
XLA Modules:
  0.0 77.9 jit_solution(532536496730609406)
XLA Ops:
  0.0 77.2 %shard_map.145 = bf16[32,16,128]{2,1,0:T(8,128)(2,1)S(1)} custom-call(bf16[32,16,128]{2,1,0:T(8,128)(2,1)} %pair_hbm.1, s32[16,32]{1,0:T(8,128)} %bitcast.6, f32[1,128]{1,0:T(1,128)} %bitcast.8, bf16[128,256]{1,0:T(8,128)(2,1)} %w_left_hbm.1, bf16[128,256]{1,0:T(8,128)(2,1)} %w_right_hbm.1, bf16[128,128]{1,0:T(8,128)(2,1)} %w_tri_gate_hbm.1, ...), custom_call_target="tpu_custom_call" | custom-call | tf_op jit(solution)/shard_map/pallas_call | solution.py:470
  77.2 0.7 copy.17

commit v6 on v4

--- a/solution.py
+++ b/solution.py
@@ -60,10 +60,10 @@
     pair_ref, mask_ref, gain_tri, w_left, w_right, w_tri_gate, gain_mid, w_tri_out, gain_att,
     w_attend, w_bias, w_attend_out, gain_trans, w_trans_in, w_trans_out, load_sems,
     work, edge_send, edge_recv, edge_work, near_all, far_all, gate_tri, tri_work, tri_send,
-    tri_recv, bias_send, bias_recv, bias_work, bias_all, bias_full, mask_cols, pair_one_t, gate_att,
+    tri_recv, mask_send, mask_recv, bias_send, bias_recv, bias_work, bias_all, bias_full, mask_cols, pair_one_t, gate_att,
     qkv_send, qkv_recv, query_buf, key_buf, value_buf, att_send, att_recv,
     edge_ss, edge_rs, near_ss, near_rs, far_ss, far_rs, tri_ss, tri_rs, bias_ss, bias_rs,
-    biasz_ss, biasz_rs, biasy_ss, biasy_rs, qkv_ss, qkv_rs, att_ss, att_rs,
+    biasc_ss, biasc_rs, pair_ss, pair_rs, mask_ss, mask_rs, qkv_ss, qkv_rs, att_ss, att_rs,
 ):
     r = lax.axis_index("row")
     c = lax.axis_index("col")
@@ -209,13 +209,38 @@
         near_all, near_ss, near_rs, ZS, z,
         ((r, y * ZS + ((z + 1) & (ZS - 1))), (r, y * ZS + ((z + ZS - 1) & (ZS - 1)))),
     )
-    bias_ring = Ring(bias_all, biasy_ss, biasy_rs, YS, y, y_ring)
     far_ring.start()
     near_ring.start()
+    sub = lax.broadcasted_iota(jnp.int32, (16, 128), 0)
+    for g in range(4):
+        part = jnp.broadcast_to(mask[:, 128 * g : 128 * g + 128], (16, 128)).astype(BF16)
+        for h in range(HEADS):
+            mask_send[4 * h + g] = part
+    mask_recv[r] = mask_send[r]
+
+    @pl.loop(1, ROWS)
+    def _(s):
+        to = (r + s) & (ROWS - 1)
+        send(mask_send.at[to], mask_recv.at[r], mask_ss.at[to], mask_rs.at[r], to, c)
+
     far_ring.turn(1)
     near_ring.turn(1, (0,))
     far_ring.turn(2)
     near_ring.turn(1, (1,))
+
+    @pl.loop(1, ROWS)
+    def _(s):
+        of = (r + s) & (ROWS - 1)
+        wait(mask_recv.at[of], mask_rs.at[of])
+
+    pieces = [
+        jnp.concatenate([mask_recv[4 * a + b].astype(F32)[:8] for a in range(4)], 0)
+        for b in range(4)
+    ]
+    for q, piece in enumerate(swap_blocks(pieces, 32)):
+        for a in range(4):
+            mask_cols[q, :, 128 * a : 128 * a + 128] = piece[8 * a : 8 * a + 8]
+
     far_ring.turn(3)
     near_ring.turn(2)
     def reply(slot, piece):
@@ -296,7 +321,6 @@
 
     normed_two = layer_norm(pair_t, gain_att[...]).astype(BF16)
     bias_t = dot(w_bias[...], normed_two, 1, 1)
-    sub = lax.broadcasted_iota(jnp.int32, (16, 128), 0)
     for h in range(HEADS):
         base = jnp.zeros((16, 128), F32)
         for v in range(4):
@@ -305,15 +329,24 @@
                 jnp.broadcast_to(bias_t[h : h + 1, 128 * v : 128 * v + 128], (16, 128)),
                 base,
             )
-        for g in range(4):
-            row = jnp.broadcast_to(mask[:, 128 * g : 128 * g + 128], (16, 128))
-            bias_send[4 * h + g] = jnp.where(sub == 4, row, base).astype(BF16)
-    bias_recv[r] = bias_send[r]
-
-    @pl.loop(1, ROWS)
-    def _(s):
-        to = (r + s) & (ROWS - 1)
-        send(bias_send.at[to], bias_recv.at[r], bias_ss.at[to], bias_rs.at[r], to, c)
+        bias_send[h] = base.astype(BF16)
+    upper = r >> 3
+    half = r & 1
+
+    @pl.loop(0, 8)
+    def _(s):
+        m = ((r >> 1) + s) & 7
+        to = 2 * m + upper
+
+        @pl.when(to != r)
+        def _():
+            send(
+                bias_send.at[m >> 1], bias_recv.at[r & 7], bias_ss.at[m], bias_rs.at[r & 7], to, c
+            )
+
+        @pl.when(to == r)
+        def _():
+            bias_recv[r & 7] = bias_send[m >> 1]
 
     projected = dot(w_attend[...], normed_two, 0, 1)
     for h in range(HEADS):
@@ -334,41 +367,52 @@
 
     gate_att[...] = jax.nn.sigmoid(projected[384:])
 
-    @pl.loop(1, ROWS)
-    def _(s):
-        of = (r + s) & (ROWS - 1)
-        wait(bias_recv.at[of], bias_rs.at[of])
+    @pl.loop(0, 8)
+    def _(s):
+        @pl.when(8 * half + s != r)
+        def _():
+            wait(bias_recv.at[s], bias_rs.at[s])
 
     pieces = [
-        jnp.concatenate([bias_recv[4 * a + b].astype(F32) for a in range(4)], 0) for b in range(4)
+        jnp.concatenate([bias_recv[4 * a + b].astype(F32)[:8] for a in range(2)], 0)
+        for b in range(4)
     ]
     for q, piece in enumerate(swap_blocks(pieces, 32)):
-        for a in range(4):
+        for a in range(2):
             for v in range(4):
-                bias_work[a, 4 * v + q : 4 * v + q + 1, :] = piece[16 * a + v : 16 * a + v + 1]
-            mask_cols[q, 0:1, 128 * a : 128 * a + 128] = piece[16 * a + 4 : 16 * a + 5]
-    for a in range(4):
-        bias_all[y, z, :, 128 * a : 128 * a + 128] = bias_work[a].astype(BF16)
-
-    @pl.loop(1, ZS)
-    def _(s):
-        to = (z + s) & (ZS - 1)
-        send(bias_all.at[y, z], bias_all.at[y, z], biasz_ss.at[to], biasz_rs.at[z], r, y * ZS + to)
-
-    @pl.loop(1, ZS)
-    def _(s):
-        of = (z + s) & (ZS - 1)
-        wait(bias_all.at[y, of], biasz_rs.at[of])
-
-    bias_ring.start()
-    bias_ring.turn(1)
+                bias_work[a, 4 * v + q : 4 * v + q + 1, :] = piece[8 * a + v : 8 * a + v + 1]
+    for a in range(2):
+        bias_all[half, c, :, 128 * a : 128 * a + 128] = bias_work[a].astype(BF16)
+
+    for near in (0, 1, 7, 2, 6, 3, 5, 4):
+        for t in range(ZS):
+            if near or t:
+                to = ((y + near) & (YS - 1)) * ZS + ((z + t) & (ZS - 1))
+                part = bias_all.at[half, c]
+                send(part, part, biasc_ss.at[to], biasc_rs.at[c], r, to)
 
     @pl.loop(1, ROWS)
     def _(s):
         of = (r + s) & (ROWS - 1)
         wait(qkv_recv.at[of], qkv_rs.at[of])
 
-    bias_ring.turn(2)
+    side = 1 - 2 * (y & 1)
+    order = [((y >> 1) + 4 + apart) & 3 for apart in (0, -side, side, 2)]
+
+    def hand_over(a):
+        @pl.loop(0, 8)
+        def _(s):
+            of = 8 * a + s
+
+            @pl.when(of != c)
+            def _():
+                wait(bias_all.at[half, of], biasc_rs.at[of])
+
+        part = bias_all.at[half, pl.ds(8 * a, 8)]
+        send(part, part, pair_ss.at[a], pair_rs.at[half, a], r ^ 1, c)
+
+    hand_over(order[0])
+
     tail = (lax.broadcasted_iota(jnp.int32, (16, 512), 0) == 0).astype(BF16)
     for q in range(4):
         value_buf[q, 32:48, :] = tail
@@ -380,12 +424,14 @@
             key_buf[q, :, 128 * a : 128 * a + 128] = piece[32:64]
             value_buf[q, 0:32, 128 * a : 128 * a + 128] = piece[64:]
 
-    side = 1 - 2 * (y & 1)
-    for step, apart in enumerate((0, -side, side, 2)):
-        if step in (1, 3):
-            bias_ring.turn(3 + step // 2)
-        a = ((y >> 1) + 4 + apart) & 3
-        bias_full[...] = bias_all[pl.ds(2 * a, 2)].astype(F32).reshape(128, 512) * LOG2E
+    for step, a in enumerate(order):
+        if step < 3:
+            hand_over(order[step + 1])
+        wait(bias_all.at[1 - half, pl.ds(8 * a, 8)], pair_rs.at[1 - half, a])
+        for s in range(2):
+            bias_full[:, 256 * s : 256 * s + 256] = (
+                bias_all[s, pl.ds(8 * a, 8)].astype(F32).reshape(128, 256) * LOG2E
+            )
         pieces = []
         for q in range(4):
             scores = dot(query_buf[q, a], key_buf[q], 0, 0) + bias_full[...]
@@ -432,14 +478,24 @@
     def _(s):
         to = (r + s) & (ROWS - 1)
         wait(edge_send.at[to], edge_ss.at[to])
-        wait(bias_send.at[to], bias_ss.at[to])
+        wait(mask_send.at[to], mask_ss.at[to])
         wait(qkv_send.at[to], qkv_ss.at[to])
         wait(att_send.at[to], att_ss.at[to])
 
-    @pl.loop(1, ZS)
-    def _(s):
-        to = (z + s) & (ZS - 1)
-        wait(bias_all.at[0, 0], biasz_ss.at[to])
+    @pl.loop(0, 8)
+    def _(s):
+        @pl.when(2 * s + upper != r)
+        def _():
+            wait(bias_send.at[s >> 1], bias_ss.at[s])
+
+    @pl.loop(0, YS * ZS)
+    def _(s):
+        @pl.when(s != c)
+        def _():
+            wait(bias_all.at[half, c], biasc_ss.at[s])
+
+    for a in range(4):
+        wait(bias_all.at[half, pl.ds(8 * a, 8)], pair_ss.at[a])
 
     @pl.loop(0, YS)
     def _(s):
@@ -449,7 +505,7 @@
             def _():
                 wait(tri_send.at[s, t], tri_ss.at[s, t])
 
-    for each in (far_ring, near_ring, bias_ring):
+    for each in (far_ring, near_ring):
         each.sent()
 
 
@@ -494,8 +550,10 @@
             pltpu.VMEM((2, 16, 16, 128), BF16),
             pltpu.VMEM((16, 16, 128), BF16),
             pltpu.VMEM((16, 16, 128), BF16),
-            pltpu.VMEM((4, 16, 128), F32),
-            pltpu.VMEM((YS, ZS, 16, 512), BF16),
+            pltpu.VMEM((4, 16, 128), BF16),
+            pltpu.VMEM((8, 16, 128), BF16),
+            pltpu.VMEM((2, 16, 128), F32),
+            pltpu.VMEM((2, YS * ZS, 16, 256), BF16),
             pltpu.VMEM((128, 512), F32),
             pltpu.VMEM((4, 8, 512), F32),
             pltpu.VMEM((512, 128), F32),
@@ -511,9 +569,10 @@
             dma((2, 5, 2)), dma((2, 5, 2)),
             dma((2, 5, 2)), dma((2, 5, 2)),
             dma((YS, ZS)), dma((2, 16)),
+            dma((8,)), dma((8,)),
+            dma((YS * ZS,)), dma((YS * ZS,)),
+            dma((4,)), dma((2, 4)),
             dma((16,)), dma((16,)),
-            dma((ZS,)), dma((ZS,)),
-            dma((2, 5, 2)), dma((2, 5, 2)),
             dma((16,)), dma((16,)),
             dma((16,)), dma((16,)),
         ],

time: 76.5 us -> 72 us (0.941)
  Pallas kernels: 75.7 us -> 71.2 us
    pallas_call x1, Pallas kernels: 75.7 us -> 71.2 us  [per_device(): pl.pallas_call(kernel, out_shape=pltpu.VMEM((32, 16, 128), BF16), in_spec...]
where the time goes in v6:
time: 72 us; the launch traced here: 71.9 us
  Pallas kernels  71.2 us (99%)
    pallas_call x1, Pallas kernels, per_device(): pl.pallas_call(kernel, out_shape=pltpu.VMEM((32, 16, 128), BF16), in_spec...  71.2 us

profile of v6, /device:TPU:65, one launch (start us, length us, event | category | flops | bytes accessed | tf_op | source)
XLA Modules:
  0.0 71.9 jit_solution(15910356220511644214)
XLA Ops:
  0.0 71.2 %shard_map.145 = bf16[32,16,128]{2,1,0:T(8,128)(2,1)S(1)} custom-call(bf16[32,16,128]{2,1,0:T(8,128)(2,1)} %pair_hbm.1, s32[16,32]{1,0:T(8,128)} %bitcast.6, f32[1,128]{1,0:T(1,128)} %bitcast.8, bf16[128,256]{1,0:T(8,128)(2,1)} %w_left_hbm.1, bf16[128,256]{1,0:T(8,128)(2,1)} %w_right_hbm.1, bf16[128,128]{1,0:T(8,128)(2,1)} %w_tri_gate_hbm.1, ...), custom_call_target="tpu_custom_call" | custom-call | tf_op jit(solution)/shard_map/pallas_call | solution.py:519
  71.2 0.7 copy.17

commit v7 on v6

--- a/solution.py
+++ b/solution.py
@@ -164,12 +164,16 @@
         far_all[y, :, :, 128 * a : 128 * a + 128] = block[1]
 
     class Ring:
-        def __init__(self, buf, ss, rs, size, me, to):
+        def __init__(self, buf, ss, rs, size, me, to, pieces):
             self.buf, self.ss, self.rs, self.size, self.me, self.to = buf, ss, rs, size, me, to
-            self.half = buf.shape[1] // 2
+            self.pieces, self.extent = pieces, buf.shape[1] // pieces
 
         def part(self, block, chunk):
-            return self.buf.at[block & (self.size - 1), pl.ds(chunk * self.half, self.half)]
+            at = block & (self.size - 1)
+            return self.buf.at[at, pl.ds(chunk * self.extent, self.extent)]
+
+        def takes(self, step, chunk, way):
+            return step < self.size // 2 or 2 * chunk // self.pieces == way
 
         def send(self, step, chunk, way):
             block = self.me + self.size - step + 1 if way == 0 else self.me + step - 1
@@ -181,33 +185,33 @@
             block = self.me + self.size - step if way == 0 else self.me + step
             wait(self.part(block, chunk), self.rs.at[way, step, chunk])
 
+        def each(self, step, chunks=None):
+            for chunk in range(self.pieces) if chunks is None else chunks:
+                for way in range(2):
+                    if self.takes(step, chunk, way):
+                        yield chunk, way
+
         def start(self):
-            for chunk in range(2):
-                for way in range(2):
-                    self.send(1, chunk, way)
-
-        def turn(self, step, chunks=(0, 1)):
-            last = self.size // 2
-            for chunk in chunks:
-                for way in range(2):
-                    if step == last and way != chunk:
-                        continue
-                    self.land(step, chunk, way)
-                    if step < last - 1 or (step == last - 1 and way == chunk):
-                        self.send(step + 1, chunk, way)
+            for chunk, way in self.each(1):
+                self.send(1, chunk, way)
+
+        def turn(self, step, chunks=None):
+            for chunk, way in self.each(step, chunks):
+                self.land(step, chunk, way)
+                if step < self.size // 2 and self.takes(step + 1, chunk, way):
+                    self.send(step + 1, chunk, way)
 
         def sent(self):
             for step in range(1, self.size // 2 + 1):
-                for chunk in range(2):
-                    for way in range(2):
-                        if step < self.size // 2 or way == chunk:
-                            wait(self.part(0, 0), self.ss.at[way, step, chunk])
+                for chunk, way in self.each(step):
+                    wait(self.part(0, 0), self.ss.at[way, step, chunk])
 
     y_ring = ((r, up), (r, down))
-    far_ring = Ring(far_all, far_ss, far_rs, YS, y, y_ring)
+    far_ring = Ring(far_all, far_ss, far_rs, YS, y, y_ring, 4)
     near_ring = Ring(
         near_all, near_ss, near_rs, ZS, z,
         ((r, y * ZS + ((z + 1) & (ZS - 1))), (r, y * ZS + ((z + ZS - 1) & (ZS - 1)))),
+        2,
     )
     far_ring.start()
     near_ring.start()
@@ -391,11 +395,6 @@
                 part = bias_all.at[half, c]
                 send(part, part, biasc_ss.at[to], biasc_rs.at[c], r, to)
 
-    @pl.loop(1, ROWS)
-    def _(s):
-        of = (r + s) & (ROWS - 1)
-        wait(qkv_recv.at[of], qkv_rs.at[of])
-
     side = 1 - 2 * (y & 1)
     order = [((y >> 1) + 4 + apart) & 3 for apart in (0, -side, side, 2)]
 
@@ -412,6 +411,12 @@
         send(part, part, pair_ss.at[a], pair_rs.at[half, a], r ^ 1, c)
 
     hand_over(order[0])
+    hand_over(order[1])
+
+    @pl.loop(1, ROWS)
+    def _(s):
+        of = (r + s) & (ROWS - 1)
+        wait(qkv_recv.at[of], qkv_rs.at[of])
 
     tail = (lax.broadcasted_iota(jnp.int32, (16, 512), 0) == 0).astype(BF16)
     for q in range(4):
@@ -425,8 +430,8 @@
             value_buf[q, 0:32, 128 * a : 128 * a + 128] = piece[64:]
 
     for step, a in enumerate(order):
-        if step < 3:
-            hand_over(order[step + 1])
+        if step < 2:
+            hand_over(order[step + 2])
         wait(bias_all.at[1 - half, pl.ds(8 * a, 8)], pair_rs.at[1 - half, a])
         for s in range(2):
             bias_full[:, 256 * s : 256 * s + 256] = (
@@ -434,10 +439,15 @@
             )
         pieces = []
         for q in range(4):
-            scores = dot(query_buf[q, a], key_buf[q], 0, 0) + bias_full[...]
-            scores = jnp.where(mask_cols[q, 0:1, :] > 0.5, scores, MASKED)
-            weight = jnp.exp2(scores - jnp.max(scores, 1, keepdims=True)).astype(BF16)
-            total = dot(value_buf[q], weight, 1, 1)
+            raw = dot(query_buf[q, a], key_buf[q], 0, 0)
+            present = mask_cols[q, 0:1, :] > 0.5
+            weights = []
+            for t in range(0, 128, 32):
+                scores = raw[t : t + 32] + bias_full[t : t + 32, :]
+                scores = jnp.where(present, scores, MASKED)
+                top = jnp.max(scores, 1, keepdims=True)
+                weights.append(jnp.exp2(scores - top).astype(BF16))
+            total = dot(value_buf[q], jnp.concatenate(weights, 0), 1, 1)
             pieces.append(total[:32] / total[32:33])
         for b, piece in enumerate(swap_blocks(pieces, 32)):
             at = 4 * a + b
@@ -469,7 +479,15 @@
     for part in range(4):
         rows = slice(128 * part, 128 * part + 128)
         expanded = dot(normed_three[rows], w_trans_in[...], 1, 0)
-        hidden = (jax.nn.silu(expanded[:, :512]) * expanded[:, 512:]).astype(BF16)
+        hidden = jnp.concatenate(
+            [
+                (
+                    jax.nn.silu(expanded[t : t + 16, :512]) * expanded[t : t + 16, 512:]
+                ).astype(BF16)
+                for t in range(0, 128, 16)
+            ],
+            0,
+        )
         work[rows, :] = pair_two[rows] + dot(hidden, w_trans_out[...], 1, 0)
     for i in range(32):
         out_ref[i] = work[pl.ds(i, 16, stride=32), :].astype(BF16)
@@ -567,7 +585,7 @@
             pltpu.VMEM((16, 32, 128), BF16),
             dma((16,)), dma((16,)),
             dma((2, 5, 2)), dma((2, 5, 2)),
-            dma((2, 5, 2)), dma((2, 5, 2)),
+            dma((2, 5, 4)), dma((2, 5, 4)),
             dma((YS, ZS)), dma((2, 16)),
             dma((8,)), dma((8,)),
             dma((YS * ZS,)), dma((YS * ZS,)),

time: 72 us -> 71.5 us (level)
  the two profiles are of different devices: /device:TPU:65 before, /device:TPU:73 now
where the time goes in v7:
time: 71.5 us; the launch traced here: 71.4 us
  Pallas kernels  70.7 us (99%)
    pallas_call x1, Pallas kernels, per_device(): pl.pallas_call(kernel, out_shape=pltpu.VMEM((32, 16, 128), BF16), in_spec...  70.7 us

profile of v7, /device:TPU:73, one launch (start us, length us, event | category | flops | bytes accessed | tf_op | source)
XLA Modules:
  0.0 71.4 jit_solution(11284089688195085410)
XLA Ops:
  0.0 70.7 %shard_map.145 = bf16[32,16,128]{2,1,0:T(8,128)(2,1)S(1)} custom-call(bf16[32,16,128]{2,1,0:T(8,128)(2,1)} %pair_hbm.1, s32[16,32]{1,0:T(8,128)} %bitcast.6, f32[1,128]{1,0:T(1,128)} %bitcast.8, bf16[128,256]{1,0:T(8,128)(2,1)} %w_left_hbm.1, bf16[128,256]{1,0:T(8,128)(2,1)} %w_right_hbm.1, bf16[128,128]{1,0:T(8,128)(2,1)} %w_tri_gate_hbm.1, ...), custom_call_target="tpu_custom_call" | custom-call | tf_op jit(solution)/shard_map/pallas_call | solution.py:537
  70.7 0.7 copy.17

commit v8 on v7

--- a/solution.py
+++ b/solution.py
@@ -11,7 +11,7 @@
 HEADS = 4
 HEAD_DIM = 32
 EPS = 1e-05
-MASKED = -1000000000.0
+MASKED = -1e30
 LOG2E = math.log2(math.e)
 ROWS = 16
 YS = 8
@@ -94,7 +94,7 @@
             ]
         )
     ]
-    for load in loads:
+    for load in loads[:5]:
         load.start()
 
     barrier = pltpu.get_barrier_semaphore()
@@ -112,6 +112,9 @@
 
     hello(r, up)
     hello(r, down)
+
+    for load in loads[5:]:
+        load.start()
 
     for load in loads[:5]:
         load.wait()
@@ -134,19 +137,15 @@
 
     pl.semaphore_wait(barrier, (ROWS - 1) + (ZS - 1) + 2)
 
-    @pl.loop(1, ROWS)
-    def _(s):
+    for s in range(1, ROWS):
         to = (r + s) & (ROWS - 1)
-        send(edge_send.at[to], edge_recv.at[r], edge_ss.at[to], edge_rs.at[r], to, c)
+        send(edge_send.at[to], edge_recv.at[r], edge_ss, edge_rs, to, c)
 
     for load in loads[5:]:
         load.wait()
     gate_tri[...] = jax.nn.sigmoid(dot(normed_t, w_tri_gate[...], 1, 0))
 
-    @pl.loop(1, ROWS)
-    def _(s):
-        of = (r + s) & (ROWS - 1)
-        wait(edge_recv.at[of], edge_rs.at[of])
+    wait(edge_recv.at[pl.ds(0, ROWS - 1)], edge_rs)
 
     for v in range(4):
         pieces = [
@@ -179,7 +178,7 @@
             block = self.me + self.size - step + 1 if way == 0 else self.me + step - 1
             part = self.part(block, chunk)
             row, col = self.to[way]
-            send(part, part, self.ss.at[way, step, chunk], self.rs.at[way, step, chunk], row, col)
+            send(part, part, self.ss, self.rs.at[way, step, chunk], row, col)
 
         def land(self, step, chunk, way):
             block = self.me + self.size - step if way == 0 else self.me + step
@@ -202,9 +201,7 @@
                     self.send(step + 1, chunk, way)
 
         def sent(self):
-            for step in range(1, self.size // 2 + 1):
-                for chunk, way in self.each(step):
-                    wait(self.part(0, 0), self.ss.at[way, step, chunk])
+            wait(self.buf.at[pl.ds(0, self.size - 1)], self.ss)
 
     y_ring = ((r, up), (r, down))
     far_ring = Ring(far_all, far_ss, far_rs, YS, y, y_ring, 4)
@@ -222,20 +219,16 @@
             mask_send[4 * h + g] = part
     mask_recv[r] = mask_send[r]
 
-    @pl.loop(1, ROWS)
-    def _(s):
+    for s in range(1, ROWS):
         to = (r + s) & (ROWS - 1)
-        send(mask_send.at[to], mask_recv.at[r], mask_ss.at[to], mask_rs.at[r], to, c)
+        send(mask_send.at[to], mask_recv.at[r], mask_ss, mask_rs, to, c)
 
     far_ring.turn(1)
     near_ring.turn(1, (0,))
     far_ring.turn(2)
     near_ring.turn(1, (1,))
 
-    @pl.loop(1, ROWS)
-    def _(s):
-        of = (r + s) & (ROWS - 1)
-        wait(mask_recv.at[of], mask_rs.at[of])
+    wait(mask_recv.at[pl.ds(0, ROWS - 1)], mask_rs)
 
     pieces = [
         jnp.concatenate([mask_recv[4 * a + b].astype(F32)[:8] for a in range(4)], 0)
@@ -255,20 +248,20 @@
         for t in (1, 2, 3):
             zz = (z + t) & (ZS - 1)
             send(
-                tri_send.at[yy, zz], tri_recv.at[half, r], tri_ss.at[yy, zz], tri_rs.at[half, r],
+                tri_send.at[yy, zz], tri_recv.at[half, r], tri_ss, tri_rs,
                 row, y * ZS + zz,
             )
 
         @pl.when(row != r)
         def _():
             send(
-                tri_send.at[yy, z], tri_recv.at[half, r], tri_ss.at[yy, z], tri_rs.at[half, r],
+                tri_send.at[yy, z], tri_recv.at[half, r], tri_ss, tri_rs,
                 row, c,
             )
 
         @pl.when(row == r)
         def _():
-            tri_recv[half, r] = tri_send[yy, z]
+            pltpu.make_async_copy(tri_send.at[yy, z], tri_recv.at[half, r], tri_rs).start()
 
     def products(slots):
         for ch in range(8):
@@ -293,13 +286,11 @@
         merged = jnp.where(lane == m, pltpu.roll(pieces[m], 16 * m, 1), merged)
     reply(7, merged)
 
-    @pl.loop(0, ROWS)
-    def _(s):
-        for half in range(2):
-
-            @pl.when(jnp.logical_or(s != r, z != 2 * (r & 1) + half))
-            def _():
-                wait(tri_recv.at[half, s], tri_rs.at[half, s])
+    wait(edge_send.at[pl.ds(0, ROWS - 1)], edge_ss)
+    wait(mask_send.at[pl.ds(0, ROWS - 1)], mask_ss)
+    far_ring.sent()
+    near_ring.sent()
+    wait(tri_recv, tri_rs)
 
     tri_t = jnp.concatenate(
         [
@@ -337,20 +328,20 @@
     upper = r >> 3
     half = r & 1
 
-    @pl.loop(0, 8)
-    def _(s):
+    own = bias_send.at[r >> 2]
+    mine = bias_recv.at[r & 7]
+
+    @pl.when(upper != half)
+    def _():
+        send(own, mine, bias_ss, bias_rs, r ^ 1, c)
+
+    @pl.when(upper == half)
+    def _():
+        pltpu.make_async_copy(own, mine, bias_rs).start()
+
+    for s in range(1, 8):
         m = ((r >> 1) + s) & 7
-        to = 2 * m + upper
-
-        @pl.when(to != r)
-        def _():
-            send(
-                bias_send.at[m >> 1], bias_recv.at[r & 7], bias_ss.at[m], bias_rs.at[r & 7], to, c
-            )
-
-        @pl.when(to == r)
-        def _():
-            bias_recv[r & 7] = bias_send[m >> 1]
+        send(bias_send.at[m >> 1], mine, bias_ss, bias_rs, 2 * m + upper, c)
 
     projected = dot(w_attend[...], normed_two, 0, 1)
     for h in range(HEADS):
@@ -364,18 +355,13 @@
                 ].astype(BF16)
     qkv_recv[r] = qkv_send[r]
 
-    @pl.loop(1, ROWS)
-    def _(s):
+    for s in range(1, ROWS):
         to = (r + s) & (ROWS - 1)
-        send(qkv_send.at[to], qkv_recv.at[r], qkv_ss.at[to], qkv_rs.at[r], to, c)
+        send(qkv_send.at[to], qkv_recv.at[r], qkv_ss, qkv_rs, to, c)
 
     gate_att[...] = jax.nn.sigmoid(projected[384:])
 
-    @pl.loop(0, 8)
-    def _(s):
-        @pl.when(8 * half + s != r)
-        def _():
-            wait(bias_recv.at[s], bias_rs.at[s])
+    wait(bias_recv, bias_rs)
 
     pieces = [
         jnp.concatenate([bias_recv[4 * a + b].astype(F32)[:8] for a in range(2)], 0)
@@ -393,61 +379,49 @@
             if near or t:
                 to = ((y + near) & (YS - 1)) * ZS + ((z + t) & (ZS - 1))
                 part = bias_all.at[half, c]
-                send(part, part, biasc_ss.at[to], biasc_rs.at[c], r, to)
+                send(part, part, biasc_ss, biasc_rs.at[c >> 3], r, to)
 
     side = 1 - 2 * (y & 1)
     order = [((y >> 1) + 4 + apart) & 3 for apart in (0, -side, side, 2)]
 
-    def hand_over(a):
-        @pl.loop(0, 8)
-        def _(s):
-            of = 8 * a + s
-
-            @pl.when(of != c)
-            def _():
-                wait(bias_all.at[half, of], biasc_rs.at[of])
-
+    def hand_over(a, count=8):
+        wait(bias_all.at[half, pl.ds(8 * a, count)], biasc_rs.at[a])
         part = bias_all.at[half, pl.ds(8 * a, 8)]
-        send(part, part, pair_ss.at[a], pair_rs.at[half, a], r ^ 1, c)
-
-    hand_over(order[0])
+        send(part, part, pair_ss, pair_rs.at[half, a], r ^ 1, c)
+
+    hand_over(order[0], 7)
     hand_over(order[1])
 
-    @pl.loop(1, ROWS)
-    def _(s):
-        of = (r + s) & (ROWS - 1)
-        wait(qkv_recv.at[of], qkv_rs.at[of])
+    wait(qkv_recv.at[pl.ds(0, ROWS - 1)], qkv_rs)
 
     tail = (lax.broadcasted_iota(jnp.int32, (16, 512), 0) == 0).astype(BF16)
+    first = lax.broadcasted_iota(jnp.int32, (16, 128), 0) == 0
     for q in range(4):
         value_buf[q, 32:48, :] = tail
     for a in range(4):
         pieces = [qkv_recv[4 * a + b].astype(F32) for b in range(4)]
         for q, piece in enumerate(swap_blocks(pieces, 32)):
-            piece = piece.astype(BF16)
-            query_buf[q, a] = piece[:32]
-            key_buf[q, :, 128 * a : 128 * a + 128] = piece[32:64]
-            value_buf[q, 0:32, 128 * a : 128 * a + 128] = piece[64:]
+            query_buf[q, a, 0:32, :] = piece[:32].astype(BF16)
+            query_buf[q, a, 32:48, :] = tail[:, :128]
+            value_buf[q, 0:32, 128 * a : 128 * a + 128] = piece[64:].astype(BF16)
+            present = mask_cols[q, :, 128 * a : 128 * a + 128]
+            absent = jnp.concatenate([present, present], 0) < 0.5
+            extra = jnp.where(jnp.logical_and(first, absent), MASKED, 0.0)
+            keys = jnp.concatenate([piece[32:64], extra], 0)
+            key_buf[q, 128 * a : 128 * a + 128, :] = keys.T.astype(BF16)
 
     for step, a in enumerate(order):
         if step < 2:
             hand_over(order[step + 2])
         wait(bias_all.at[1 - half, pl.ds(8 * a, 8)], pair_rs.at[1 - half, a])
         for s in range(2):
-            bias_full[:, 256 * s : 256 * s + 256] = (
-                bias_all[s, pl.ds(8 * a, 8)].astype(F32).reshape(128, 256) * LOG2E
-            )
+            block = bias_all[s, pl.ds(8 * a, 8)].astype(F32).reshape(128, 256) * LOG2E
+            bias_full[256 * s : 256 * s + 256, :] = block.T
         pieces = []
         for q in range(4):
-            raw = dot(query_buf[q, a], key_buf[q], 0, 0)
-            present = mask_cols[q, 0:1, :] > 0.5
-            weights = []
-            for t in range(0, 128, 32):
-                scores = raw[t : t + 32] + bias_full[t : t + 32, :]
-                scores = jnp.where(present, scores, MASKED)
-                top = jnp.max(scores, 1, keepdims=True)
-                weights.append(jnp.exp2(scores - top).astype(BF16))
-            total = dot(value_buf[q], jnp.concatenate(weights, 0), 1, 1)
+            scores = dot(key_buf[q], query_buf[q, a], 1, 0) + bias_full[...]
+            weight = jnp.exp2(scores - jnp.max(scores, 0, keepdims=True)).astype(BF16)
+            total = dot(value_buf[q], weight, 1, 0)
             pieces.append(total[:32] / total[32:33])
         for b, piece in enumerate(swap_blocks(pieces, 32)):
             at = 4 * a + b
@@ -455,16 +429,36 @@
 
             @pl.when(r != at)
             def _():
-                send(att_send.at[at], att_recv.at[r], att_ss.at[at], att_rs.at[r], at, c)
+                send(att_send.at[at], att_recv.at[r], att_ss, att_rs, at, c)
 
             @pl.when(r == at)
             def _():
                 att_recv[r] = att_send[at]
 
-    @pl.loop(1, ROWS)
-    def _(s):
-        of = (r + s) & (ROWS - 1)
-        wait(att_recv.at[of], att_rs.at[of])
+    @pl.when(upper != half)
+    def _():
+        wait(bias_recv, bias_ss)
+
+    @pl.when(upper == half)
+    def _():
+        wait(bias_recv.at[pl.ds(0, 7)], bias_ss)
+
+    to_self = (2 * (r >> 1) + (z >> 1)) == r
+
+    @pl.when(jnp.logical_not(to_self))
+    def _():
+        wait(tri_send, tri_ss)
+
+    @pl.when(to_self)
+    def _():
+        wait(tri_send.at[pl.ds(0, YS - 1)], tri_ss)
+        wait(tri_send.at[0, pl.ds(0, ZS - 1)], tri_ss)
+
+    wait(qkv_send.at[pl.ds(0, ROWS - 1)], qkv_ss)
+    wait(bias_all.at[half, pl.ds(0, YS * ZS - 1)], biasc_ss)
+    wait(bias_all.at[half], pair_ss)
+    wait(att_send.at[pl.ds(0, ROWS - 1)], att_ss)
+    wait(att_recv.at[pl.ds(0, ROWS - 1)], att_rs)
 
     attended = jnp.concatenate(
         [
@@ -491,40 +485,6 @@
         work[rows, :] = pair_two[rows] + dot(hidden, w_trans_out[...], 1, 0)
     for i in range(32):
         out_ref[i] = work[pl.ds(i, 16, stride=32), :].astype(BF16)
-
-    @pl.loop(1, ROWS)
-    def _(s):
-        to = (r + s) & (ROWS - 1)
-        wait(edge_send.at[to], edge_ss.at[to])
-        wait(mask_send.at[to], mask_ss.at[to])
-        wait(qkv_send.at[to], qkv_ss.at[to])
-        wait(att_send.at[to], att_ss.at[to])
-
-    @pl.loop(0, 8)
-    def _(s):
-        @pl.when(2 * s + upper != r)
-        def _():
-            wait(bias_send.at[s >> 1], bias_ss.at[s])
-
-    @pl.loop(0, YS * ZS)
-    def _(s):
-        @pl.when(s != c)
-        def _():
-            wait(bias_all.at[half, c], biasc_ss.at[s])
-
-    for a in range(4):
-        wait(bias_all.at[half, pl.ds(8 * a, 8)], pair_ss.at[a])
-
-    @pl.loop(0, YS)
-    def _(s):
-        for t in range(ZS):
-
-            @pl.when(jnp.logical_or(2 * s + (z >> 1) != r, z != t))
-            def _():
-                wait(tri_send.at[s, t], tri_ss.at[s, t])
-
-    for each in (far_ring, near_ring):
-        each.sent()
 
 
 def per_device(
@@ -572,27 +532,27 @@
             pltpu.VMEM((8, 16, 128), BF16),
             pltpu.VMEM((2, 16, 128), F32),
             pltpu.VMEM((2, YS * ZS, 16, 256), BF16),
-            pltpu.VMEM((128, 512), F32),
+            pltpu.VMEM((512, 128), F32),
             pltpu.VMEM((4, 8, 512), F32),
             pltpu.VMEM((512, 128), F32),
             pltpu.VMEM((128, 512), F32),
             pltpu.VMEM((16, 96, 128), BF16),
             pltpu.VMEM((16, 96, 128), BF16),
-            pltpu.VMEM((4, 4, 32, 128), BF16),
-            pltpu.VMEM((4, 32, 512), BF16),
+            pltpu.VMEM((4, 4, 48, 128), BF16),
+            pltpu.VMEM((4, 512, 48), BF16),
             pltpu.VMEM((4, 48, 512), BF16),
             pltpu.VMEM((16, 32, 128), BF16),
             pltpu.VMEM((16, 32, 128), BF16),
-            dma((16,)), dma((16,)),
-            dma((2, 5, 2)), dma((2, 5, 2)),
-            dma((2, 5, 4)), dma((2, 5, 4)),
-            dma((YS, ZS)), dma((2, 16)),
-            dma((8,)), dma((8,)),
-            dma((YS * ZS,)), dma((YS * ZS,)),
-            dma((4,)), dma((2, 4)),
-            dma((16,)), dma((16,)),
-            dma((16,)), dma((16,)),
-            dma((16,)), dma((16,)),
+            dma(()), dma(()),
+            dma(()), dma((2, 3, 2)),
+            dma(()), dma((2, 5, 4)),
+            dma(()), dma(()),
+            dma(()), dma(()),
+            dma(()), dma((4,)),
+            dma(()), dma((2, 4)),
+            dma(()), dma(()),
+            dma(()), dma(()),
+            dma(()), dma(()),
         ],
         compiler_params=pltpu.CompilerParams(
             collective_id=0, has_side_effects=True, vmem_limit_bytes=VMEM_LIMIT

time: 71.5 us -> 67.1 us (0.938)
  the two profiles are of different devices: /device:TPU:73 before, /device:TPU:65 now
where the time goes in v8:
time: 67.1 us; the launch traced here: 67 us
  Pallas kernels  66.3 us (99%)
    pallas_call x1, Pallas kernels, per_device(): pl.pallas_call(kernel, out_shape=pltpu.VMEM((32, 16, 128), BF16), in_spec...  66.3 us

profile of v8, /device:TPU:65, one launch (start us, length us, event | category | flops | bytes accessed | tf_op | source)
XLA Modules:
  0.0 67.0 jit_solution(3825220092755364797)
XLA Ops:
  0.0 66.3 %shard_map.145 = bf16[32,16,128]{2,1,0:T(8,128)(2,1)S(1)} custom-call(bf16[32,16,128]{2,1,0:T(8,128)(2,1)} %pair_hbm.1, s32[16,32]{1,0:T(8,128)} %bitcast.6, f32[1,128]{1,0:T(1,128)} %bitcast.8, bf16[128,256]{1,0:T(8,128)(2,1)} %w_left_hbm.1, bf16[128,256]{1,0:T(8,128)(2,1)} %w_right_hbm.1, bf16[128,128]{1,0:T(8,128)(2,1)} %w_tri_gate_hbm.1, ...), custom_call_target="tpu_custom_call" | custom-call | tf_op jit(solution)/shard_map/pallas_call | solution.py:497
  66.3 0.7 copy.17

commit v9 on v8

--- a/solution.py
+++ b/solution.py
@@ -133,13 +133,12 @@
         projected = dot(weight[...], normed_t, 0, 1)
         sides.append((mask * jax.nn.sigmoid(projected[:128]) * projected[128:]).reshape(ROWS, 8, 512))
     edge_send[...] = jnp.concatenate(sides, 1).astype(BF16)
-    edge_recv[r] = edge_send[r]
-
     pl.semaphore_wait(barrier, (ROWS - 1) + (ZS - 1) + 2)
 
     for s in range(1, ROWS):
         to = (r + s) & (ROWS - 1)
         send(edge_send.at[to], edge_recv.at[r], edge_ss, edge_rs, to, c)
+    edge_recv[r] = edge_send[r]
 
     for load in loads[5:]:
         load.wait()
@@ -204,7 +203,7 @@
             wait(self.buf.at[pl.ds(0, self.size - 1)], self.ss)
 
     y_ring = ((r, up), (r, down))
-    far_ring = Ring(far_all, far_ss, far_rs, YS, y, y_ring, 4)
+    far_ring = Ring(far_all, far_ss, far_rs, YS, y, y_ring, 2)
     near_ring = Ring(
         near_all, near_ss, near_rs, ZS, z,
         ((r, y * ZS + ((z + 1) & (ZS - 1))), (r, y * ZS + ((z + ZS - 1) & (ZS - 1)))),
@@ -252,6 +251,11 @@
                 row, y * ZS + zz,
             )
 
+    def reply_here(slot):
+        yy = (y + YS + slot - 3) & (YS - 1)
+        row = 2 * yy + (z >> 1)
+        half = z & 1
+
         @pl.when(row != r)
         def _():
             send(
@@ -278,6 +282,8 @@
     pieces = swap_blocks(products(range(7)), 16)
     for slot in (2, 4, 1, 5, 0, 6, 3):
         reply(slot, pieces[slot])
+    for slot in (2, 4, 1, 5, 0, 6, 3):
+        reply_here(slot)
     far_ring.turn(4)
     pieces = products([7])
     lane = lax.broadcasted_iota(jnp.int32, pieces[0].shape, 1) >> 4
@@ -285,6 +291,7 @@
     for m in range(1, 8):
         merged = jnp.where(lane == m, pltpu.roll(pieces[m], 16 * m, 1), merged)
     reply(7, merged)
+    reply_here(7)
 
     wait(edge_send.at[pl.ds(0, ROWS - 1)], edge_ss)
     wait(mask_send.at[pl.ds(0, ROWS - 1)], mask_ss)
@@ -353,11 +360,10 @@
                 qkv_send[4 * h + g, 32 * part : 32 * part + 32, :] = rows[
                     :, 128 * g : 128 * g + 128
                 ].astype(BF16)
-    qkv_recv[r] = qkv_send[r]
-
     for s in range(1, ROWS):
         to = (r + s) & (ROWS - 1)
         send(qkv_send.at[to], qkv_recv.at[r], qkv_ss, qkv_rs, to, c)
+    qkv_recv[r] = qkv_send[r]
 
     gate_att[...] = jax.nn.sigmoid(projected[384:])
 
@@ -411,8 +417,6 @@
             key_buf[q, 128 * a : 128 * a + 128, :] = keys.T.astype(BF16)
 
     for step, a in enumerate(order):
-        if step < 2:
-            hand_over(order[step + 2])
         wait(bias_all.at[1 - half, pl.ds(8 * a, 8)], pair_rs.at[1 - half, a])
         for s in range(2):
             block = bias_all[s, pl.ds(8 * a, 8)].astype(F32).reshape(128, 256) * LOG2E
@@ -424,16 +428,22 @@
             total = dot(value_buf[q], weight, 1, 0)
             pieces.append(total[:32] / total[32:33])
         for b, piece in enumerate(swap_blocks(pieces, 32)):
-            at = 4 * a + b
-            att_send[at] = piece.astype(BF16)
-
-            @pl.when(r != at)
-            def _():
-                send(att_send.at[at], att_recv.at[r], att_ss, att_rs, at, c)
-
-            @pl.when(r == at)
-            def _():
-                att_recv[r] = att_send[at]
+            att_send[4 * a + b] = piece.astype(BF16)
+        for t in (1, 2, 3):
+            at = 4 * a + ((r + t) & 3)
+            send(att_send.at[at], att_recv.at[r], att_ss, att_rs, at, c)
+        at = 4 * a + (r & 3)
+
+        @pl.when(r != at)
+        def _():
+            send(att_send.at[at], att_recv.at[r], att_ss, att_rs, at, c)
+
+        @pl.when(r == at)
+        def _():
+            att_recv[r] = att_send[at]
+
+        if step < 2:
+            hand_over(order[step + 2])
 
     @pl.when(upper != half)
     def _():
@@ -545,7 +555,7 @@
             pltpu.VMEM((16, 32, 128), BF16),
             dma(()), dma(()),
             dma(()), dma((2, 3, 2)),
-            dma(()), dma((2, 5, 4)),
+            dma(()), dma((2, 5, 2)),
             dma(()), dma(()),
             dma(()), dma(()),
             dma(()), dma((4,)),

time: 67.1 us -> 67.4 us (level)
  no operation moved by 1% of the time
where the time goes in v9:
time: 67.4 us; the launch traced here: 67.2 us
  Pallas kernels  66.6 us (99%)
    pallas_call x1, Pallas kernels, per_device(): pl.pallas_call(kernel, out_shape=pltpu.VMEM((32, 16, 128), BF16), in_spec...  66.6 us

profile of v9, /device:TPU:65, one launch (start us, length us, event | category | flops | bytes accessed | tf_op | source)
XLA Modules:
  0.0 67.2 jit_solution(4798756040382251759)
XLA Ops:
  0.0 66.6 %shard_map.145 = bf16[32,16,128]{2,1,0:T(8,128)(2,1)S(1)} custom-call(bf16[32,16,128]{2,1,0:T(8,128)(2,1)} %pair_hbm.1, s32[16,32]{1,0:T(8,128)} %bitcast.6, f32[1,128]{1,0:T(1,128)} %bitcast.8, bf16[128,256]{1,0:T(8,128)(2,1)} %w_left_hbm.1, bf16[128,256]{1,0:T(8,128)(2,1)} %w_right_hbm.1, bf16[128,128]{1,0:T(8,128)(2,1)} %w_tri_gate_hbm.1, ...), custom_call_target="tpu_custom_call" | custom-call | tf_op jit(solution)/shard_map/pallas_call | solution.py:507
  66.6 0.7 copy.17

commit v10 on v9

--- a/solution.py
+++ b/solution.py
@@ -63,7 +63,7 @@
     tri_recv, mask_send, mask_recv, bias_send, bias_recv, bias_work, bias_all, bias_full, mask_cols, pair_one_t, gate_att,
     qkv_send, qkv_recv, query_buf, key_buf, value_buf, att_send, att_recv,
     edge_ss, edge_rs, near_ss, near_rs, far_ss, far_rs, tri_ss, tri_rs, bias_ss, bias_rs,
-    biasc_ss, biasc_rs, pair_ss, pair_rs, mask_ss, mask_rs, qkv_ss, qkv_rs, att_ss, att_rs,
+    biasz_ss, biasz_rs, biasc_ss, biasc_rs, pair_ss, pair_rs, mask_ss, mask_rs, qkv_ss, qkv_rs, att_ss, att_rs,
 ):
     r = lax.axis_index("row")
     c = lax.axis_index("col")
@@ -380,12 +380,14 @@
     for a in range(2):
         bias_all[half, c, :, 128 * a : 128 * a + 128] = bias_work[a].astype(BF16)
 
-    for near in (0, 1, 7, 2, 6, 3, 5, 4):
-        for t in range(ZS):
-            if near or t:
-                to = ((y + near) & (YS - 1)) * ZS + ((z + t) & (ZS - 1))
-                part = bias_all.at[half, c]
-                send(part, part, biasc_ss, biasc_rs.at[c >> 3], r, to)
+    for t in (1, 2, 3):
+        part = bias_all.at[half, c]
+        send(part, part, biasz_ss, biasz_rs, r, y * ZS + ((z + t) & (ZS - 1)))
+    four = bias_all.at[half, pl.ds(y * ZS, ZS)]
+    wait(bias_all.at[half, pl.ds(0, ZS - 1)], biasz_rs)
+    for near in (1, 7, 2, 6, 3, 5, 4):
+        to = ((y + near) & (YS - 1)) * ZS + z
+        send(four, four, biasc_ss, biasc_rs.at[y >> 1], r, to)
 
     side = 1 - 2 * (y & 1)
     order = [((y >> 1) + 4 + apart) & 3 for apart in (0, -side, side, 2)]
@@ -395,7 +397,7 @@
         part = bias_all.at[half, pl.ds(8 * a, 8)]
         send(part, part, pair_ss, pair_rs.at[half, a], r ^ 1, c)
 
-    hand_over(order[0], 7)
+    hand_over(order[0], 4)
     hand_over(order[1])
 
     wait(qkv_recv.at[pl.ds(0, ROWS - 1)], qkv_rs)
@@ -465,7 +467,8 @@
         wait(tri_send.at[0, pl.ds(0, ZS - 1)], tri_ss)
 
     wait(qkv_send.at[pl.ds(0, ROWS - 1)], qkv_ss)
-    wait(bias_all.at[half, pl.ds(0, YS * ZS - 1)], biasc_ss)
+    wait(bias_all.at[half, pl.ds(0, ZS - 1)], biasz_ss)
+    wait(bias_all.at[half, pl.ds(0, (YS - 1) * ZS)], biasc_ss)
     wait(bias_all.at[half], pair_ss)
     wait(att_send.at[pl.ds(0, ROWS - 1)], att_ss)
     wait(att_recv.at[pl.ds(0, ROWS - 1)], att_rs)
@@ -558,6 +561,7 @@
             dma(()), dma((2, 5, 2)),
             dma(()), dma(()),
             dma(()), dma(()),
+            dma(()), dma(()),
             dma(()), dma((4,)),
             dma(()), dma((2, 4)),
             dma(()), dma(()),

time: 67.4 us -> 68.8 us (1.021)
  Pallas kernels: 66.6 us -> 67.7 us
    pallas_call x1, Pallas kernels: 66.6 us -> 67.7 us  [per_device(): pl.pallas_call(kernel, out_shape=pltpu.VMEM((32, 16, 128), BF16), in_spec...]
where the time goes in v10:
time: 68.8 us; the launch traced here: 68.4 us
  Pallas kernels  67.7 us (98%)
    pallas_call x1, Pallas kernels, per_device(): pl.pallas_call(kernel, out_shape=pltpu.VMEM((32, 16, 128), BF16), in_spec...  67.7 us

profile of v10, /device:TPU:65, one launch (start us, length us, event | category | flops | bytes accessed | tf_op | source)
XLA Modules:
  0.0 68.4 jit_solution(17299951690552747115)
XLA Ops:
  0.0 67.7 %shard_map.145 = bf16[32,16,128]{2,1,0:T(8,128)(2,1)S(1)} custom-call(bf16[32,16,128]{2,1,0:T(8,128)(2,1)} %pair_hbm.1, s32[16,32]{1,0:T(8,128)} %bitcast.6, f32[1,128]{1,0:T(1,128)} %bitcast.8, bf16[128,256]{1,0:T(8,128)(2,1)} %w_left_hbm.1, bf16[128,256]{1,0:T(8,128)(2,1)} %w_right_hbm.1, bf16[128,128]{1,0:T(8,128)(2,1)} %w_tri_gate_hbm.1, ...), custom_call_target="tpu_custom_call" | custom-call | tf_op jit(solution)/shard_map/pallas_call | solution.py:510
  67.7 0.7 copy.17
